TPU v7x, 32 devices: a whole 2x2x4 slice. The times are simulated.
32 devices in a mesh: round: 4 (over y, x), bucket: 8 (over z, core).
Axes of the slice: x: 2, y: 2, z: 4, core: 2. Of those that a mesh axis runs over, the one named last changes fastest.
Arguments:
- x_start: float32 [4, 4096, 512], P('round', 'bucket'), may hold values from 0 to 1
- y_start: float32 [4, 4096, 512], P('round', 'bucket'), may hold values from 0 to 1
- bucket_payoff: bfloat16 [4, 4096, 4096], P('round', 'bucket'), may hold values from -0.09375 to 0.09375
- column_blocks: int32 [4, 4, 3], P('round'), may hold values from 0 to 3
- public_coef: float32 [4, 4, 3, 128, 128], P('round'), may hold values from -0.3125 to 0.3125
- predecessor_sequences: int32 [3, 256], replicated, may hold values from 0 to 511, as said below
Outputs:
- x_final: float32 [4, 4096, 512], P('round', 'bucket')
- y_final: float32 [4, 4096, 512], P('round', 'bucket')
Inputs may be any that keep to these rules, and one draw needn't show every extreme that they name: `predecessor_sequences`: each row names 256 distinct sequences of the previous round.
All inputs are finite; a program needn't handle non-finite values.
Results may differ from a plain program's by a relative error of at most 0.013.
The roundings to bfloat16 on the way count: a program that leaves them out, or rounds other values in their place, can miss the bound.
Values may be sent and summed in bfloat16 or wider, within the bound.
A program may use at most 64 MiB of HBM per device.

v0:
```python
import functools

import jax
import jax.numpy as jnp
from jax import lax
from jax.experimental import pallas as pl
from jax.experimental.pallas import tpu as pltpu
from jax.sharding import PartitionSpec as P

smooth_x = 0.1
smooth_y = 0.1
epsilon = 1e-06
highest = lax.Precision.HIGHEST
nn = (((1,), (0,)), ((), ()))
nt = (((1,), (1,)), ((), ()))


def exact(a, b, dims=nn):
    return lax.dot_general(a, b, dims, precision=highest, preferred_element_type=jnp.float32)


def kernel(
    n_r,
    n_b,
    x_ref,
    y_ref,
    pay_ref,
    col_ref,
    coef_ref,
    pred_ref,
    xo_ref,
    yo_ref,
    xs,
    ys,
    mixer,
    gather,
    pay_t,
    blocks,
    mixed,
    grad,
    sib_out,
    sib_in,
    far_out,
    far_in,
    sq_b,
    sq_r,
    rows_in,
    score,
    norm,
    mass,
    back_in,
    far_q,
    far_s,
    far_q_in,
    far_s_in,
    row_q,
    row_s,
    row_q_in,
    row_s_in,
    back_q,
    back_s,
    back_q_in,
    back_s_in,
    ag_send,
    ag_recv,
    fw_send,
    line_send,
    sib_send,
    sib_recv,
    far_send,
    far_recv,
    sqb_send,
    sqb_recv,
    sqr_send,
    sqr_recv,
    row_send,
    row_recv,
    back_send,
    back_recv,
    far_s_send,
    far_s_recv,
    row_s_send,
    row_s_recv,
    back_s_send,
    back_s_recv,
):
    rows, seqs = xs.shape
    half = seqs // 2
    part = rows // n_r
    pairs = n_b // 2
    me_r = lax.axis_index("round")
    me_b = lax.axis_index("bucket")
    pair = me_b // 2
    core = me_b % 2
    sibling = pair * 2 + 1 - core
    total_count = n_r * n_b * rows * seqs

    def remote(src, dst, send, recv, **where):
        return pltpu.make_async_remote_copy(
            src_ref=src,
            dst_ref=dst,
            send_sem=send,
            recv_sem=recv,
            device_id=where,
            device_id_type=pl.DeviceIdType.MESH,
        )

    barrier = pltpu.get_barrier_semaphore()
    for d in range(1, n_b):
        pl.semaphore_signal(
            barrier,
            inc=1,
            device_id={"bucket": (me_b + d) % n_b},
            device_id_type=pl.DeviceIdType.MESH,
        )
    for d in range(1, n_r):
        pl.semaphore_signal(
            barrier,
            inc=1,
            device_id={"round": (me_r + d) % n_r},
            device_id_type=pl.DeviceIdType.MESH,
        )
    pl.semaphore_wait(barrier, n_b + n_r - 2)

    def order(i):
        return jnp.where(i < half, 2 * i, 2 * (i - half) + 1)

    down = lax.broadcasted_iota(jnp.int32, (seqs, seqs), 0)
    across = lax.broadcasted_iota(jnp.int32, (seqs, seqs), 1)
    to_inner = (down == order(across)).astype(jnp.float32)
    to_outer = (order(down) == across).astype(jnp.float32)

    tiles, per_row, tile, _ = coef_ref.shape[1:]
    for m in range(tiles):
        for c in range(tiles):
            value = jnp.zeros((tile, tile), jnp.float32)
            for t in range(per_row):
                value = value + jnp.where(col_ref[0, m, t] == c, coef_ref[0, m, t], 0.0)
            mixer[m * tile : (m + 1) * tile, c * tile : (c + 1) * tile] = value
    mixer[...] = exact(to_outer, exact(mixer[...], to_inner))
    ys[...] = exact(y_ref[0], to_inner)
    for r in range(n_r - 1):
        place = order(lax.broadcasted_iota(jnp.int32, (seqs, half), 0))
        gather[r] = (place == pred_ref[r : r + 1, :]).astype(jnp.float32)

    def columns(j):
        return pl.ds(pl.multiple_of(j * rows, rows), rows)

    def coded(value, code_ref, scale_ref):
        top = jnp.max(jnp.abs(value), axis=0, keepdims=True)
        unit = jnp.maximum(top, 1e-30) / 32767.0
        code = jnp.floor(value * (1.0 / unit) + 0.5)
        code_ref[...] = code.astype(jnp.int32).astype(jnp.int16)
        scale_ref[...] = jnp.broadcast_to(unit, scale_ref.shape)

    def decoded(code_ref, scale_ref):
        return code_ref[...].astype(jnp.int32).astype(jnp.float32) * scale_ref[0:1, :]

    def prox(state, sign, factor, weight, short):
        def row_copy(d):
            s = (me_r + d) % n_r
            here = grad.at[pl.ds(pl.multiple_of(s * part, part), part)]
            if not short:
                return [
                    remote(here, rows_in.at[me_r], row_send.at[s], row_recv.at[me_r], round=s)
                ]
            return [
                remote(
                    row_q.at[s], row_q_in.at[me_r], row_send.at[s], row_recv.at[me_r], round=s
                ),
                remote(
                    row_s.at[s], row_s_in.at[me_r], row_s_send.at[s], row_s_recv.at[me_r], round=s
                ),
            ]

        def row_arrival(d):
            s = (me_r + d) % n_r
            if not short:
                return [
                    remote(rows_in.at[s], rows_in.at[s], row_send.at[s], row_recv.at[s], round=s)
                ]
            return [
                remote(row_q_in.at[s], row_q_in.at[s], row_send.at[s], row_recv.at[s], round=s),
                remote(
                    row_s_in.at[s], row_s_in.at[s], row_s_send.at[s], row_s_recv.at[s], round=s
                ),
            ]

        for d in range(1, n_r):
            if short:
                s = (me_r + d) % n_r
                here = pl.ds(pl.multiple_of(s * part, part), part)
                coded(grad[here, :], row_q.at[s], row_s.at[s])
            for copy in row_copy(d):
                copy.start()
        squares = grad[...]
        squares = jnp.sum((squares * squares).reshape(rows // 8, 8, seqs), axis=0)
        squares = sum(squares[:, i * 128 : (i + 1) * 128] for i in range(seqs // 128))
        sq_b[me_b] = squares

        def sqb_copy(d):
            s = (me_b + d) % n_b
            return remote(
                sq_b.at[me_b], sq_b.at[me_b], sqb_send.at[d], sqb_recv.at[me_b], bucket=s
            )

        def sqb_arrival(d):
            s = (me_b + d) % n_b
            return remote(sq_b.at[s], sq_b.at[s], sqb_send.at[d], sqb_recv.at[s], bucket=s)

        for d in range(1, n_b):
            sqb_copy(d).start()
        rows_in[me_r] = grad[pl.ds(pl.multiple_of(me_r * part, part), part), :]
        for d in range(1, n_b):
            sqb_arrival(d).wait_recv()
        sq_r[me_r] = jnp.sum(sq_b[...], axis=0)

        def sqr_copy(d):
            s = (me_r + d) % n_r
            return remote(sq_r.at[me_r], sq_r.at[me_r], sqr_send.at[d], sqr_recv.at[me_r], round=s)

        def sqr_arrival(d):
            s = (me_r + d) % n_r
            return remote(sq_r.at[s], sq_r.at[s], sqr_send.at[d], sqr_recv.at[s], round=s)

        for d in range(1, n_r):
            sqr_copy(d).start()
        for d in range(1, n_r):
            sqr_arrival(d).wait_recv()
        squares = jnp.sum(jnp.sum(sq_r[...], axis=0), axis=0, keepdims=True)
        squares = jnp.sum(squares, axis=1, keepdims=True)
        scale = sign / (factor * jnp.sqrt(squares / total_count + epsilon))
        for d in range(1, n_r):
            for copy in row_arrival(d):
                copy.wait_recv()
            if short:
                s = (me_r + d) % n_r
                rows_in[s] = decoded(row_q_in.at[s], row_s_in.at[s])

        for r in reversed(range(n_r)):
            values = rows_in[r] * scale
            if r < n_r - 1:
                values = values + exact(norm[r + 1], gather[r], nt)
            score[r] = values
            even, odd = values[:, :half], values[:, half:]
            larger = jnp.maximum(even, odd)
            norm[r] = larger + jnp.log(jnp.exp(even - larger) + jnp.exp(odd - larger))

        def back_copy(r):
            if not short:
                return [
                    remote(
                        mass.at[r], back_in.at[me_r], back_send.at[r], back_recv.at[me_r], round=r
                    )
                ]
            return [
                remote(
                    back_q.at[r], back_q_in.at[me_r], back_send.at[r], back_recv.at[me_r], round=r
                ),
                remote(
                    back_s.at[r],
                    back_s_in.at[me_r],
                    back_s_send.at[r],
                    back_s_recv.at[me_r],
                    round=r,
                ),
            ]

        def back_arrival(s):
            if not short:
                return [
                    remote(
                        back_in.at[s], back_in.at[s], back_send.at[s], back_recv.at[s], round=s
                    )
                ]
            return [
                remote(
                    back_q_in.at[s], back_q_in.at[s], back_send.at[s], back_recv.at[s], round=s
                ),
                remote(
                    back_s_in.at[s], back_s_in.at[s], back_s_send.at[s], back_s_recv.at[s], round=s
                ),
            ]

        for r in range(n_r):
            even = jnp.exp(score[r, :, :half] - norm[r])
            odd = jnp.exp(score[r, :, half:] - norm[r])
            if r > 0:
                parent = exact(mass[r - 1], gather[r - 1])
                even = parent * even
                odd = parent * odd
            mass[r, :, :half] = even
            mass[r, :, half:] = odd

            @pl.when(me_r != r)
            def _():
                if short:
                    coded(mass[r], back_q.at[r], back_s.at[r])
                for copy in back_copy(r):
                    copy.start()

        def update(s, best):
            here = pl.ds(pl.multiple_of(s * part, part), part)
            state[here, :] = (1.0 - weight) * state[here, :] + weight * best

        update(me_r, mass[me_r])
        for d in range(1, n_r):
            s = (me_r + d) % n_r
            for copy in back_arrival(s):
                copy.wait_recv()
            if short:
                update(s, decoded(back_q_in.at[s], back_s_in.at[s]))
            else:
                update(s, back_in[s])
        for d in range(1, n_r):
            for copy in row_copy(d) + back_copy((me_r + d) % n_r):
                copy.wait_send()
            sqr_copy(d).wait_send()
        for d in range(1, n_b):
            sqb_copy(d).wait_send()

    def step(index, _):
        weight = 2.0 / (index.astype(jnp.float32) + 3.0)
        short = False

        blocks[me_b] = exact(ys[...], mixer[...], nt).astype(jnp.bfloat16)

        def own_copy(kind):
            target = (sibling, me_b + 2, me_b - 2)[kind]
            return remote(
                blocks.at[me_b], blocks.at[me_b], ag_send.at[kind], ag_recv.at[me_b], bucket=target
            )

        def go_on(b, d, step):
            return remote(
                blocks.at[b], blocks.at[b], line_send.at[d], ag_recv.at[b], bucket=me_b + step
            )

        def pass_on(b, d):
            return remote(blocks.at[b], blocks.at[b], fw_send.at[d], ag_recv.at[b], bucket=sibling)

        def arrival(b):
            return remote(
                blocks.at[b], blocks.at[b], ag_send.at[0], ag_recv.at[b], bucket=sibling
            )

        def product(b):
            return jnp.dot(
                pay_ref[0, :, columns(b)], blocks[b], preferred_element_type=jnp.float32
            )

        @pl.when(pair < pairs - 1)
        def _():
            own_copy(1).start()

        @pl.when(pair > 0)
        def _():
            own_copy(2).start()

        own_copy(0).start()
        @pl.when(index == 0)
        def _():
            xs[...] = exact(x_ref[0], to_inner)

            def turn(j, _):
                pay_t[columns(j), :] = pay_ref[0, :, columns(j)].T
                return 0

            lax.fori_loop(0, n_b, turn, 0)
        grad[...] = product(me_b)
        arrival(sibling).wait_recv()
        grad[...] += product(sibling)

        def take(d, _):
            left = me_b - 2 * d
            right = me_b + 2 * d

            @pl.when(pair >= d)
            def _():
                arrival(left).wait_recv()

                @pl.when(pair < pairs - 1)
                def _():
                    go_on(left, d, 2).start()

                pass_on(left, d).start()

            @pl.when(pair + d < pairs)
            def _():
                arrival(right).wait_recv()

                @pl.when(pair > 0)
                def _():
                    go_on(right, pairs + d, -2).start()

                pass_on(right, pairs + d).start()

            def use(b, other):
                grad[...] += product(b)
                arrival(other).wait_recv()
                grad[...] += product(other)

            @pl.when(pair >= d)
            def _():
                use(left, sibling - 2 * d)

            @pl.when(pair + d < pairs)
            def _():
                use(right, sibling + 2 * d)

            return 0

        lax.fori_loop(1, pairs, take, 0)

        def drain(d, _):
            left = me_b - 2 * d
            right = me_b + 2 * d

            @pl.when(pair >= d)
            def _():
                pass_on(left, d).wait_send()

                @pl.when(pair < pairs - 1)
                def _():
                    go_on(left, d, 2).wait_send()

            @pl.when(pair + d < pairs)
            def _():
                pass_on(right, pairs + d).wait_send()

                @pl.when(pair > 0)
                def _():
                    go_on(right, pairs + d, -2).wait_send()

            return 0

        lax.fori_loop(1, pairs, drain, 0)
        own_copy(0).wait_send()

        @pl.when(pair < pairs - 1)
        def _():
            own_copy(1).wait_send()

        @pl.when(pair > 0)
        def _():
            own_copy(2).wait_send()

        prox(xs, -1.0, smooth_x, weight, short)

        mixed[...] = exact(xs[...], mixer[...]).astype(jnp.bfloat16)

        def partial(b):
            return jnp.dot(pay_t[columns(b), :], mixed[...], preferred_element_type=jnp.float32)

        def sib_copy(q):
            return remote(
                sib_out.at[q], sib_in.at[q], sib_send.at[q], sib_recv.at[q], bucket=sibling
            )

        def far_copy(q, step, target):
            slot = q if step > 0 else pairs + q
            if not short:
                return [
                    remote(
                        far_out.at[q],
                        far_in.at[slot],
                        far_send.at[q],
                        far_recv.at[slot],
                        bucket=target,
                    )
                ]
            return [
                remote(
                    far_q.at[q],
                    far_q_in.at[slot],
                    far_send.at[q],
                    far_recv.at[slot],
                    bucket=target,
                ),
                remote(
                    far_s.at[q],
                    far_s_in.at[slot],
                    far_s_send.at[q],
                    far_s_recv.at[slot],
                    bucket=target,
                ),
            ]

        def far_value(q, step):
            slot = q if step > 0 else pairs + q
            for copy in far_copy(q, step, sibling):
                copy.wait_recv()
            if short:
                return decoded(far_q_in.at[slot], far_s_in.at[slot])
            return far_in[slot]

        def to_sibling(q):
            sib_out[q] = partial(q * 2 + 1 - core)
            sib_copy(q).start()

        def move(q, step):
            far_out[q] = partial(q * 2 + core)
            sib_copy(q).wait_recv()
            far_out[q] += sib_in[q]

            @pl.when(pair > 0 if step > 0 else pair < pairs - 1)
            def _():
                far_out[q] += far_value(q, step)

            if short:
                coded(far_out[q], far_q.at[q], far_s.at[q])
            for copy in far_copy(q, step, me_b + step):
                copy.start()

        def outward(right, left):
            def one(i, _):
                @pl.when(pair < pairs - 1 - i)
                def _():
                    right(pairs - 1 - i)

                @pl.when(pair > i)
                def _():
                    left(i)

                return 0

            lax.fori_loop(0, pairs - 1, one, 0)

        def far_done(q, step):
            for copy in far_copy(q, step, me_b + step):
                copy.wait_send()

        outward(to_sibling, to_sibling)
        outward(lambda q: move(q, 2), lambda q: move(q, -2))
        to_sibling(pair)
        grad[...] = partial(me_b)
        sib_copy(pair).wait_recv()
        grad[...] += sib_in[pair]

        @pl.when(pair > 0)
        def _():
            grad[...] += far_value(pair, 2)

        @pl.when(pair < pairs - 1)
        def _():
            grad[...] += far_value(pair, -2)

        outward(lambda q: far_done(q, 2), lambda q: far_done(q, -2))
        for q in range(pairs):
            sib_copy(q).wait_send()
        prox(ys, 1.0, smooth_y, weight, short)
        return 0

    lax.fori_loop(0, 2, step, 0)
    down = lax.broadcasted_iota(jnp.int32, (seqs, seqs), 0)
    across = lax.broadcasted_iota(jnp.int32, (seqs, seqs), 1)
    to_outer = (order(down) == across).astype(jnp.float32)
    xo_ref[0] = exact(xs[...], to_outer)
    yo_ref[0] = exact(ys[...], to_outer)


def body(x_start, y_start, bucket_payoff, column_blocks, public_coef, predecessor_sequences):
    n_r = lax.axis_size("round")
    n_b = lax.axis_size("bucket")
    _, rows, seqs = x_start.shape
    part = rows // n_r
    pairs = n_b // 2
    f32, bf16 = jnp.float32, jnp.bfloat16
    vmem = pl.BlockSpec(memory_space=pltpu.VMEM)
    smem = pl.BlockSpec(memory_space=pltpu.SMEM)
    dma = pltpu.SemaphoreType.DMA
    return pl.pallas_call(
        functools.partial(kernel, n_r, n_b),
        out_shape=[jax.ShapeDtypeStruct(x_start.shape, f32)] * 2,
        in_specs=[vmem, vmem, vmem, smem, vmem, vmem],
        out_specs=[vmem, vmem],
        scratch_shapes=[
            pltpu.VMEM((rows, seqs), f32),
            pltpu.VMEM((rows, seqs), f32),
            pltpu.VMEM((seqs, seqs), f32),
            pltpu.VMEM((n_r - 1, seqs, seqs // 2), f32),
            pltpu.VMEM((n_b * rows, rows), bf16),
            pltpu.VMEM((n_b, rows, seqs), bf16),
            pltpu.VMEM((rows, seqs), bf16),
            pltpu.VMEM((rows, seqs), f32),
            pltpu.VMEM((pairs, rows, seqs), f32),
            pltpu.VMEM((pairs, rows, seqs), f32),
            pltpu.VMEM((pairs, rows, seqs), f32),
            pltpu.VMEM((2 * pairs, rows, seqs), f32),
            pltpu.VMEM((n_b, 8, 128), f32),
            pltpu.VMEM((n_r, 8, 128), f32),
            pltpu.VMEM((n_r, part, seqs), f32),
            pltpu.VMEM((n_r, part, seqs), f32),
            pltpu.VMEM((n_r, part, seqs // 2), f32),
            pltpu.VMEM((n_r, part, seqs), f32),
            pltpu.VMEM((n_r, part, seqs), f32),
            pltpu.VMEM((16, 128), jnp.int16),
            pltpu.VMEM((pairs, 8, seqs), f32),
            pltpu.VMEM((16, 128), jnp.int16),
            pltpu.VMEM((2 * pairs, 8, seqs), f32),
            pltpu.VMEM((16, 128), jnp.int16),
            pltpu.VMEM((n_r, 8, seqs), f32),
            pltpu.VMEM((16, 128), jnp.int16),
            pltpu.VMEM((n_r, 8, seqs), f32),
            pltpu.VMEM((16, 128), jnp.int16),
            pltpu.VMEM((n_r, 8, seqs), f32),
            pltpu.VMEM((16, 128), jnp.int16),
            pltpu.VMEM((n_r, 8, seqs), f32),
            dma((3,)),
            dma((n_b,)),
            dma((2 * pairs,)),
            dma((2 * pairs,)),
            dma((pairs,)),
            dma((pairs,)),
            dma((pairs,)),
            dma((2 * pairs,)),
            dma((n_b,)),
            dma((n_b,)),
            dma((n_r,)),
            dma((n_r,)),
            dma((n_r,)),
            dma((n_r,)),
            dma((n_r,)),
            dma((n_r,)),
            dma((pairs,)),
            dma((2 * pairs,)),
            dma((n_r,)),
            dma((n_r,)),
            dma((n_r,)),
            dma((n_r,)),
        ],
        compiler_params=pltpu.CompilerParams(
            collective_id=0, has_side_effects=True, vmem_limit_bytes=60 * 1024 * 1024
        ),
    )(x_start, y_start, bucket_payoff, column_blocks, public_coef, predecessor_sequences)


def solution(mesh):
    in_specs = (
        P("round", "bucket", None),
        P("round", "bucket", None),
        P("round", "bucket", None),
        P("round", None, None),
        P("round", None, None, None, None),
        P(),
    )
    out_specs = (P("round", "bucket", None), P("round", "bucket", None))

    def run(*arrays):
        return tuple(
            jax.shard_map(
                body, mesh=mesh, in_specs=in_specs, out_specs=out_specs, check_vma=False
            )(*arrays)
        )

    return run
```

profile of v0, /device:TPU:0, one launch (start us, length us, event | category | flops | bytes accessed | tf_op | source)
XLA Modules:
  0.0 427.6 jit_solution(18322439638816110837)
XLA Ops:
  0.6 1.3 copy.8.col_ref
  2.0 421.1 %shard_map.77 = (f32[1,512,512]{2,1,0:T(8,128)}, f32[1,512,512]{2,1,0:T(8,128)}) custom-call(f32[1,512,512]{2,1,0:T(8,128)} %x_ref.1, f32[1,512,512]{2,1,0:T(8,128)} %y_ref.1, bf16[1,512,4096]{2,1,0:T(8,128)(2,1)} %pay_ref.1, s32[1,4,3]{2,1,0:T(4,128)} %copy.8.col_ref, f32[1,4,3,128,128]{4,3,2,1,0:T(8,128)} %coef_ref.1, s32[3,256]{1,0:T(4,128)} %pred_ref.1), custom_call_target="tpu_custom_call" | custom-call | tf_op jit(solution)/shard_map/pallas_call | solution.py:572
  423.1 2.3 copy.11
  425.4 2.3 copy.12
where the time goes:
time: 428 us
  Pallas kernels  421 us (98%)
  local copies, waits for them, and re-layouts  5.86 us (1%)
    pallas_call x1, Pallas kernels, body(): pl.pallas_call(functools.partial(kernel, n_r, n_b), out_shape=[jax.ShapeD...  421 us

commit v1 on v0

--- a/solution.py
+++ b/solution.py
@@ -1,4 +1,5 @@
 import functools
+import types
 
 import jax
 import jax.numpy as jnp
@@ -19,7 +20,658 @@
     return lax.dot_general(a, b, dims, precision=highest, preferred_element_type=jnp.float32)
 
 
-def kernel(
+weights = (2.0 / 3.0, 2.0 / 4.0)
+top_code = 65535.0
+shift_code = 32768
+
+
+def split3(value):
+    hi = value.astype(jnp.bfloat16)
+    left = value - hi.astype(jnp.float32)
+    mid = left.astype(jnp.bfloat16)
+    lo = (left - mid.astype(jnp.float32)).astype(jnp.bfloat16)
+    return [hi, mid, lo]
+
+
+def dot(a, b, dims=nn):
+    return lax.dot_general(a, b, dims, preferred_element_type=jnp.float32)
+
+
+def picked(parts, one_hot, dims=nn):
+    size = parts[0].shape[0]
+    out = dot(jnp.concatenate(parts, axis=0), one_hot, dims)
+    return sum(out[i * size : (i + 1) * size] for i in range(len(parts)))
+
+
+def mix(parts, factors, dims):
+    size = parts[0].shape[0]
+    total = None
+    for i, factor in reversed(list(enumerate(factors))):
+        count = min(len(parts), 3 - i)
+        out = dot(jnp.concatenate(parts[:count], axis=0), factor, dims)
+        for j in reversed(range(count)):
+            term = out[j * size : (j + 1) * size]
+            total = term if total is None else total + term
+    return total
+
+
+def encode(value, code_ref):
+    rows = value.shape[0]
+    top = jnp.maximum(jnp.max(jnp.abs(value), axis=0, keepdims=True), 1e-30)
+    power = jnp.floor(256.0 * jnp.log2(top * (1.0 / 32767.0))) + 1.0
+    code = jnp.floor(value * jnp.exp2(power * (-1.0 / 256.0)) + 0.5)
+    code_ref[:rows, :] = code.astype(jnp.int32).astype(jnp.int16)
+    power = jnp.broadcast_to(power, (16, value.shape[1]))
+    code_ref[rows:, :] = power.astype(jnp.int32).astype(jnp.int16)
+
+
+def decode(code_ref):
+    rows = code_ref.shape[0] - 16
+    power = code_ref[rows:, :].astype(jnp.int32).astype(jnp.float32)[0:1, :]
+    unit = jnp.exp2(power * (1.0 / 256.0))
+    return code_ref[:rows, :].astype(jnp.int32).astype(jnp.float32) * unit
+
+
+def line_kernel(names, n_r, n_b, *refs):
+    k = types.SimpleNamespace(**dict(zip(names, refs)))
+    f32, bf16 = jnp.float32, jnp.bfloat16
+    _, rows, seqs = k.x_hbm.shape
+    half = seqs // 2
+    wide = half // 2
+    part = rows // n_r
+    pairs = n_b // 2
+    me_r = lax.axis_index("round")
+    me_b = lax.axis_index("bucket")
+    pair = me_b // 2
+    core = me_b % 2
+    sibling = pair * 2 + 1 - core
+    inner = (pair > 0) & (pair < pairs - 1)
+    total_count = n_r * n_b * rows * seqs
+
+    def remote(src, dst, send, recv, **where):
+        return pltpu.make_async_remote_copy(
+            src_ref=src,
+            dst_ref=dst,
+            send_sem=send,
+            recv_sem=recv,
+            device_id=where,
+            device_id_type=pl.DeviceIdType.MESH,
+        )
+
+    load_y = pltpu.make_async_copy(k.y_hbm, k.yv, k.load_sem.at[0])
+    load_pay = pltpu.make_async_copy(k.pay_hbm, k.pay, k.load_sem.at[1])
+    load_x = pltpu.make_async_copy(k.x_hbm, k.xv, k.load_sem.at[2])
+    load_y.start()
+    load_pay.start()
+    load_x.start()
+
+    barrier = pltpu.get_barrier_semaphore()
+    for d in range(1, n_b):
+        pl.semaphore_signal(
+            barrier,
+            inc=1,
+            device_id={"bucket": (me_b + d) % n_b},
+            device_id_type=pl.DeviceIdType.MESH,
+        )
+    for d in range(1, n_r):
+        pl.semaphore_signal(
+            barrier,
+            inc=1,
+            device_id={"round": (me_r + d) % n_r},
+            device_id_type=pl.DeviceIdType.MESH,
+        )
+
+    def order(i):
+        return 2 * (i // half * wide + i % wide) + (i % half) // wide
+
+    down = lax.broadcasted_iota(jnp.int32, (seqs, seqs), 0)
+    across = lax.broadcasted_iota(jnp.int32, (seqs, seqs), 1)
+    k.to_outer[...] = (order(down) == across).astype(f32).astype(bf16)
+
+    tiles, per_row, tile, _ = k.coef_ref.shape[1:]
+    for m in range(tiles):
+        for c in range(tiles):
+            value = jnp.zeros((tile, tile), f32)
+            for t in range(per_row):
+                value = value + jnp.where(k.col_ref[0, m, t] == c, k.coef_ref[0, m, t], 0.0)
+            k.mixer[m * tile : (m + 1) * tile, c * tile : (c + 1) * tile] = value
+    for i, piece in enumerate(split3(k.mixer[...])):
+        k.mix_p[i] = dot(k.to_outer[...], piece).astype(bf16)
+
+    def rows_of(s):
+        return pl.ds(pl.multiple_of(s * part, part), part)
+
+    def columns(j):
+        return pl.ds(pl.multiple_of(j * rows, rows), rows)
+
+
+    def own_copy(kind, s):
+        target = (sibling, me_b + 2, me_b - 2)[kind]
+        here = k.blocks.at[me_b, :, rows_of(s), :]
+        return remote(here, here, k.ag_send.at[kind, s], k.ag_recv.at[me_b, s], bucket=target)
+
+    def own_start(s):
+        @pl.when(pair < pairs - 1)
+        def _():
+            own_copy(1, s).start()
+
+        @pl.when(pair > 0)
+        def _():
+            own_copy(2, s).start()
+
+        own_copy(0, s).start()
+
+    def own_drain(s):
+        @pl.when(pair < pairs - 1)
+        def _():
+            own_copy(1, s).wait_send()
+
+        @pl.when(pair > 0)
+        def _():
+            own_copy(2, s).wait_send()
+
+        own_copy(0, s).wait_send()
+
+    def set_own(s, value):
+        value = value.astype(bf16)
+        for h in range(2):
+            k.blocks[me_b, h, rows_of(s), :] = value[:, h * half : (h + 1) * half]
+
+    load_y.wait()
+    for s in range(n_r):
+        value = mix(split3(k.yv[0, rows_of(s), :]), [k.mix_p[i] for i in range(3)], nt)
+        k.f_y[rows_of(s), :] = value
+        set_own(s, value)
+        if s == 0:
+            pl.semaphore_wait(barrier, n_b + n_r - 2)
+        own_start(s)
+
+    def by_parts(b):
+        for s in range(n_r):
+            here = k.blocks.at[b, :, rows_of(s), :]
+            remote(here, here, k.ag_send.at[0, s], k.ag_recv.at[b, s], bucket=sibling).wait_recv()
+
+    def by_half(b, h):
+        here = k.blocks.at[b, h]
+        remote(here, here, k.ag_send.at[0, h], k.ag_recv.at[b, h], bucket=sibling).wait_recv()
+
+    def go_on(b, h, step):
+        here = k.blocks.at[b, h]
+        return remote(
+            here, here, k.line_send.at[b, h], k.ag_recv.at[b, h], bucket=me_b + step
+        )
+
+    def pass_on(b, h):
+        here = k.blocks.at[b, h]
+        return remote(here, here, k.pass_send.at[b, h], k.ag_recv.at[b, h], bucket=sibling)
+
+    def product(b, h):
+        return dot(k.pay[0, :, columns(b)], k.blocks[b, h])
+
+    def setup():
+        load_pay.wait()
+
+        def turn(q, _):
+            k.pay_out[q] = k.pay[0, :, columns(q * 2 + 1 - core)].T
+            turned(q).start()
+            k.pay_t[q, core] = k.pay[0, :, columns(q * 2 + core)].T
+            return 0
+
+        lax.fori_loop(0, pairs, turn, 0)
+        for r in range(n_r - 1):
+            place = order(lax.broadcasted_iota(jnp.int32, (seqs, half), 0))
+            one_hot = (place == k.pred_ref[r : r + 1, :]).astype(f32).astype(bf16)
+            k.gather[r] = one_hot
+            k.spread[r] = one_hot.T
+        load_x.wait()
+        value = picked(split3(exact(k.xv[0], k.mixer[...])), k.to_outer[...], nt)
+        k.f_x[...] = value
+        for i in range(3):
+            k.mix_p[i] = dot(k.mix_p[i], k.to_outer[...], nt).astype(bf16)
+
+    def turned(q):
+        return remote(
+            k.pay_out.at[q],
+            k.pay_t.at[q, core],
+            k.turn_send.at[q],
+            k.turn_recv.at[q],
+            bucket=sibling,
+        )
+
+
+    def row_copy(d, h):
+        s = (me_r + d) % n_r
+        return remote(
+            k.row_q.at[s, h],
+            k.row_in.at[me_r, h],
+            k.row_send.at[s, h],
+            k.row_recv.at[me_r, h],
+            round=s,
+        )
+
+    def row_arrival(d, h):
+        s = (me_r + d) % n_r
+        here = k.row_in.at[s, h]
+        return remote(here, here, k.row_send.at[s, h], k.row_recv.at[s, h], round=s)
+
+    def finish(h):
+        for d in range(1, n_r):
+            s = (me_r + d) % n_r
+            encode(k.grad[h, rows_of(s), :], k.row_q.at[s, h])
+            row_copy(d, h).start()
+        squares = k.grad[h]
+        squares = jnp.sum((squares * squares).reshape(rows // 8, 8, half), axis=0)
+        squares = squares[:, :wide] + squares[:, wide:]
+        if h == 0:
+            k.sq_b[me_b] = squares
+        else:
+            k.sq_b[me_b] += squares
+        k.rows_f[me_r, h] = k.grad[h, rows_of(me_r), :]
+
+    def sqb_copy(d):
+        s = (me_b + d) % n_b
+        here = k.sq_b.at[me_b]
+        return remote(here, here, k.sqb_send.at[d], k.sqb_recv.at[me_b], bucket=s)
+
+    def sqb_arrival(d):
+        s = (me_b + d) % n_b
+        here = k.sq_b.at[s]
+        return remote(here, here, k.sqb_send.at[d], k.sqb_recv.at[s], bucket=s)
+
+    def sqr_copy(d):
+        s = (me_r + d) % n_r
+        here = k.sq_r.at[me_r]
+        return remote(here, here, k.sqr_send.at[d], k.sqr_recv.at[me_r], round=s)
+
+    def sqr_arrival(d):
+        s = (me_r + d) % n_r
+        here = k.sq_r.at[s]
+        return remote(here, here, k.sqr_send.at[d], k.sqr_recv.at[s], round=s)
+
+    def back_copy(r):
+        return remote(
+            k.back_q.at[r], k.back_in.at[me_r], k.back_send.at[r], k.back_recv.at[me_r], round=r
+        )
+
+    def back_arrival(s):
+        here = k.back_in.at[s]
+        return remote(here, here, k.back_send.at[s], k.back_recv.at[s], round=s)
+
+    def prox(sign, factor):
+        for d in range(1, n_b):
+            sqb_copy(d).start()
+        for d in range(1, n_r):
+            row_arrival(d, 0).wait_recv()
+            s = (me_r + d) % n_r
+            k.rows_f[s, 0] = decode(k.row_in.at[s, 0])
+        for d in range(1, n_b):
+            sqb_arrival(d).wait_recv()
+        k.sq_r[me_r] = jnp.sum(k.sq_b[...], axis=0)
+        for d in range(1, n_r):
+            sqr_copy(d).start()
+        for d in range(1, n_r):
+            row_arrival(d, 1).wait_recv()
+            s = (me_r + d) % n_r
+            k.rows_f[s, 1] = decode(k.row_in.at[s, 1])
+        for d in range(1, n_r):
+            sqr_arrival(d).wait_recv()
+        squares = jnp.sum(jnp.sum(k.sq_r[...], axis=0), axis=0, keepdims=True)
+        squares = jnp.sum(squares, axis=1, keepdims=True)
+        scale = sign / (factor * jnp.sqrt(squares / total_count + epsilon))
+
+        carried = None
+        shares = [None] * n_r
+        for r in reversed(range(n_r)):
+            norms = []
+            shares[r] = []
+            for h in range(2):
+                values = k.rows_f[r, h] * scale
+                if carried is not None:
+                    values = values + carried[:, h * half : (h + 1) * half]
+                even, odd = values[:, :wide], values[:, wide:]
+                small = jnp.exp(-jnp.abs(even - odd))
+                larger = 1.0 / (1.0 + small)
+                smaller = small * larger
+                ahead = even >= odd
+                k.share[r, h, :, :wide] = jnp.where(ahead, larger, smaller)
+                k.share[r, h, :, wide:] = jnp.where(ahead, smaller, larger)
+                norms.append(jnp.maximum(even, odd) + jnp.log(1.0 + small))
+            if r > 0:
+                norm = jnp.concatenate(norms, axis=1)
+                carried = picked(split3(norm), k.spread[r - 1])
+
+        mass = None
+        for r in range(n_r):
+            halves = []
+            if r > 0:
+                parent = picked(split3(mass), k.gather[r - 1])
+            for h in range(2):
+                now = k.share[r, h]
+                if r > 0:
+                    above = parent[:, h * wide : (h + 1) * wide]
+                    now = now * jnp.concatenate([above, above], axis=1)
+                halves.append(now)
+            mass = jnp.concatenate(halves, axis=1)
+            code = jnp.floor(mass * top_code + 0.5).astype(jnp.int32) - shift_code
+            k.back_q[r] = code.astype(jnp.int16)
+
+            @pl.when(me_r != r)
+            def _():
+                back_copy(r).start()
+
+            @pl.when(me_r == r)
+            def _():
+                k.back_in[me_r] = k.back_q[r]
+
+    def prox_drain():
+        for d in range(1, n_r):
+            for h in range(2):
+                row_copy(d, h).wait_send()
+            back_copy((me_r + d) % n_r).wait_send()
+            sqr_copy(d).wait_send()
+        for d in range(1, n_b):
+            sqb_copy(d).wait_send()
+
+    def pieces(s):
+        whole = (k.back_in[s].astype(jnp.int32) + shift_code).astype(f32)
+        hi = whole.astype(bf16)
+        return [hi, (whole - hi.astype(f32)).astype(bf16)]
+
+    def mixed_part(s, state, weight, dims):
+        value = mix(pieces(s), [k.mix_p[i] for i in range(3)], dims)
+        value = (1.0 - weight) * state[rows_of(s), :] + (weight * (1.0 / top_code)) * value
+        state[rows_of(s), :] = value
+        return value
+
+    def add_best(out, s, share):
+        best = picked(pieces(s), k.to_outer[...])
+        out[0, rows_of(s), :] += (share * (1.0 / top_code)) * best
+
+
+    def mixed_copy(s):
+        here = k.mixed.at[core, :, rows_of(s), :]
+        return remote(here, here, k.mx_send.at[s], k.mx_recv.at[core, s], bucket=sibling)
+
+    def mixed_arrival(s):
+        here = k.mixed.at[1 - core, :, rows_of(s), :]
+        return remote(here, here, k.mx_send.at[s], k.mx_recv.at[1 - core, s], bucket=sibling)
+
+    def partial(q, h):
+        return dot(k.pay_t[q, 0], k.mixed[0, h]) + dot(k.pay_t[q, 1], k.mixed[1, h])
+
+    def sum_copy(way, q, h):
+        return remote(
+            k.sum_out.at[way, q, h],
+            k.sum_in.at[way, q, h],
+            k.sum_send.at[way, q, h],
+            k.sum_recv.at[way, q, h],
+            bucket=jnp.where(way == 0, me_b + 2, me_b - 2),
+        )
+
+    def sum_arrival(way, q, h):
+        here = k.sum_in.at[way, q, h]
+        return remote(
+            here, here, k.sum_send.at[way, q, h], k.sum_recv.at[way, q, h], bucket=sibling
+        )
+
+    def sum_unit(i):
+        j = i // 2
+        up = (i % 2 == 0) == (pair < pairs // 2)
+        way = jnp.where(up, 0, 1)
+        q = jnp.where(up, pairs - 1 - j // 2, j // 2)
+        valid = jnp.where(up, q > pair, q < pair)
+        fed = jnp.where(up, pair > 0, pair < pairs - 1)
+        return way, q, j % 2, valid, fed
+
+    def step(index, _):
+        weight = 2.0 / (index.astype(f32) + 3.0)
+
+        @pl.when(index == 0)
+        def _():
+            setup()
+
+        for h in range(2):
+            k.grad[h] = product(me_b, h)
+        by_parts(sibling)
+        for h in range(2):
+            k.grad[h] += product(sibling, h)
+
+        @pl.when(index == 0)
+        def _():
+            for q in range(pairs):
+                turned(q).wait()
+            k.xo_ref[...] = (1.0 - weights[0]) * (1.0 - weights[1]) * k.xv[...]
+            k.yo_ref[...] = (1.0 - weights[0]) * (1.0 - weights[1]) * k.yv[...]
+
+        def toward(place):
+            near = jnp.where(pair % 2 == 0, 2, -2)
+            side = jnp.where(pair < pairs // 2, 1, -1)
+            second = side * jnp.where(inner, 2, 4)
+            far = side * jnp.where(inner, 4, 6)
+            return (near, second, far)[place]
+
+        def take(place):
+            offset = toward(place)
+            b, other = me_b + offset, sibling + offset
+            onward = jnp.where(offset < 0, 2, -2)
+
+            def send_on(h):
+                @pl.when(inner)
+                def _():
+                    go_on(b, h, onward).start()
+
+                pass_on(b, h).start()
+
+            if place == 0:
+                by_parts(b)
+            elif place == 1:
+
+                @pl.when(inner)
+                def _():
+                    by_parts(b)
+
+            for h in range(2):
+                if place == 1:
+
+                    @pl.when(jnp.logical_not(inner))
+                    def _():
+                        by_half(b, h)
+
+                elif place == 2:
+                    by_half(b, h)
+                send_on(h)
+                if place == 2:
+                    k.grad[h] += product(b, h)
+                    by_half(other, h)
+                    k.grad[h] += product(other, h)
+                    finish(h)
+            if place < 2:
+                for h in range(2):
+                    k.grad[h] += product(b, h)
+                    by_half(other, h)
+                    k.grad[h] += product(other, h)
+
+        def take_drain(place):
+            offset = toward(place)
+            for h in range(2):
+
+                @pl.when(inner)
+                def _():
+                    go_on(me_b + offset, h, jnp.where(offset < 0, 2, -2)).wait_send()
+
+                pass_on(me_b + offset, h).wait_send()
+
+        take(0)
+
+        @pl.when(index == 1)
+        def _():
+            for s in range(n_r):
+                add_best(k.yo_ref, s, weights[0] * (1.0 - weights[1]))
+
+        take(1)
+        take(2)
+        for place in range(3):
+            take_drain(place)
+        for s in range(n_r):
+            own_drain(s)
+
+        prox(-1.0, smooth_x)
+        for d in range(n_r):
+            s = (me_r + d) % n_r
+            if d > 0:
+                back_arrival(s).wait_recv()
+            value = mixed_part(s, k.f_x, weight, nn).astype(bf16)
+            for h in range(2):
+                k.mixed[core, h, rows_of(s), :] = value[:, h * half : (h + 1) * half]
+            mixed_copy(s).start()
+        for d in range(n_r):
+            mixed_arrival((me_r + d) % n_r).wait_recv()
+
+        def move(i, _):
+            way, q, h, valid, fed = sum_unit(i)
+
+            @pl.when(valid)
+            def _():
+                k.work[...] = partial(q, h)
+
+                @pl.when(fed)
+                def _():
+                    sum_arrival(way, q, h).wait_recv()
+                    k.work[...] += decode(k.sum_in.at[way, q, h])
+
+                encode(k.work[...], k.sum_out.at[way, q, h])
+                sum_copy(way, q, h).start()
+
+            return 0
+
+        lax.fori_loop(0, 4 * (pairs - 1), move, 0)
+        prox_drain()
+        for s in range(n_r):
+            mixed_copy(s).wait_send()
+        share = jnp.where(index == 0, weights[0] * (1.0 - weights[1]), weights[1])
+        for s in range(n_r):
+            add_best(k.xo_ref, s, share)
+        for h in range(2):
+            k.grad[h] = partial(pair, h)
+
+            @pl.when(pair > 0)
+            def _():
+                sum_arrival(0, pair, h).wait_recv()
+                k.grad[h] += decode(k.sum_in.at[0, pair, h])
+
+            @pl.when(pair < pairs - 1)
+            def _():
+                sum_arrival(1, pair, h).wait_recv()
+                k.grad[h] += decode(k.sum_in.at[1, pair, h])
+
+            finish(h)
+
+        def settle(i, _):
+            way, q, h, valid, fed = sum_unit(i)
+
+            @pl.when(valid)
+            def _():
+                sum_copy(way, q, h).wait_send()
+
+            return 0
+
+        lax.fori_loop(0, 4 * (pairs - 1), settle, 0)
+
+        prox(1.0, smooth_y)
+        for d in range(n_r):
+            s = (me_r + d) % n_r
+            if d > 0:
+                back_arrival(s).wait_recv()
+
+            @pl.when(index == 0)
+            def _():
+                set_own(s, mixed_part(s, k.f_y, weight, nt))
+                own_start(s)
+
+            @pl.when(index == 1)
+            def _():
+                add_best(k.yo_ref, s, weights[1])
+
+        prox_drain()
+        return 0
+
+    lax.fori_loop(0, 2, step, 0)
+
+
+def line_body(x_start, y_start, bucket_payoff, column_blocks, public_coef, predecessor_sequences):
+    n_r = lax.axis_size("round")
+    n_b = lax.axis_size("bucket")
+    _, rows, seqs = x_start.shape
+    half = seqs // 2
+    part = rows // n_r
+    pairs = n_b // 2
+    f32, bf16, i16 = jnp.float32, jnp.bfloat16, jnp.int16
+    vmem = pl.BlockSpec(memory_space=pltpu.VMEM)
+    smem = pl.BlockSpec(memory_space=pltpu.SMEM)
+    hbm = pl.BlockSpec(memory_space=pl.ANY)
+    dma = pltpu.SemaphoreType.DMA
+    scratch = dict(
+        xv=pltpu.VMEM((1, rows, seqs), f32),
+        yv=pltpu.VMEM((1, rows, seqs), f32),
+        pay=pltpu.VMEM((1, rows, n_b * rows), bf16),
+        pay_t=pltpu.VMEM((pairs, 2, rows, rows), bf16),
+        pay_out=pltpu.VMEM((pairs, rows, rows), bf16),
+        blocks=pltpu.VMEM((n_b, 2, rows, half), bf16),
+        mixed=pltpu.VMEM((2, 2, rows, half), bf16),
+        mixer=pltpu.VMEM((seqs, seqs), f32),
+        mix_p=pltpu.VMEM((3, seqs, seqs), bf16),
+        to_outer=pltpu.VMEM((seqs, seqs), bf16),
+        gather=pltpu.VMEM((n_r - 1, seqs, half), bf16),
+        spread=pltpu.VMEM((n_r - 1, half, seqs), bf16),
+        f_x=pltpu.VMEM((rows, seqs), f32),
+        f_y=pltpu.VMEM((rows, seqs), f32),
+        grad=pltpu.VMEM((2, rows, half), f32),
+        work=pltpu.VMEM((rows, half), f32),
+        sum_out=pltpu.VMEM((2, pairs, 2, rows + 16, half), i16),
+        sum_in=pltpu.VMEM((2, pairs, 2, rows + 16, half), i16),
+        row_q=pltpu.VMEM((n_r, 2, part + 16, half), i16),
+        row_in=pltpu.VMEM((n_r, 2, part + 16, half), i16),
+        rows_f=pltpu.VMEM((n_r, 2, part, half), f32),
+        share=pltpu.VMEM((n_r, 2, part, half), f32),
+        back_q=pltpu.VMEM((n_r, part, seqs), i16),
+        back_in=pltpu.VMEM((n_r, part, seqs), i16),
+        sq_b=pltpu.VMEM((n_b, 8, 128), f32),
+        sq_r=pltpu.VMEM((n_r, 8, 128), f32),
+        load_sem=dma((3,)),
+        turn_send=dma((pairs,)),
+        turn_recv=dma((pairs,)),
+        ag_send=dma((3, n_r)),
+        ag_recv=dma((n_b, n_r)),
+        line_send=dma((n_b, 2)),
+        pass_send=dma((n_b, 2)),
+        mx_send=dma((n_r,)),
+        mx_recv=dma((2, n_r)),
+        sum_send=dma((2, pairs, 2)),
+        sum_recv=dma((2, pairs, 2)),
+        row_send=dma((n_r, 2)),
+        row_recv=dma((n_r, 2)),
+        back_send=dma((n_r,)),
+        back_recv=dma((n_r,)),
+        sqb_send=dma((n_b,)),
+        sqb_recv=dma((n_b,)),
+        sqr_send=dma((n_r,)),
+        sqr_recv=dma((n_r,)),
+    )
+    names = ["x_hbm", "y_hbm", "pay_hbm", "col_ref", "coef_ref", "pred_ref", "xo_ref", "yo_ref"]
+    names += list(scratch)
+    return pl.pallas_call(
+        functools.partial(line_kernel, names, n_r, n_b),
+        out_shape=[jax.ShapeDtypeStruct(x_start.shape, f32)] * 2,
+        in_specs=[hbm, hbm, hbm, smem, vmem, vmem],
+        out_specs=[vmem, vmem],
+        scratch_shapes=list(scratch.values()),
+        compiler_params=pltpu.CompilerParams(
+            collective_id=0, has_side_effects=True, vmem_limit_bytes=60 * 1024 * 1024
+        ),
+    )(x_start, y_start, bucket_payoff, column_blocks, public_coef, predecessor_sequences)
+
+
+def plain_kernel(
     n_r,
     n_b,
     x_ref,
@@ -559,7 +1211,7 @@
     yo_ref[0] = exact(ys[...], to_outer)
 
 
-def body(x_start, y_start, bucket_payoff, column_blocks, public_coef, predecessor_sequences):
+def plain_body(x_start, y_start, bucket_payoff, column_blocks, public_coef, predecessor_sequences):
     n_r = lax.axis_size("round")
     n_b = lax.axis_size("bucket")
     _, rows, seqs = x_start.shape
@@ -570,7 +1222,7 @@
     smem = pl.BlockSpec(memory_space=pltpu.SMEM)
     dma = pltpu.SemaphoreType.DMA
     return pl.pallas_call(
-        functools.partial(kernel, n_r, n_b),
+        functools.partial(plain_kernel, n_r, n_b),
         out_shape=[jax.ShapeDtypeStruct(x_start.shape, f32)] * 2,
         in_specs=[vmem, vmem, vmem, smem, vmem, vmem],
         out_specs=[vmem, vmem],
@@ -646,10 +1298,12 @@
     )
     out_specs = (P("round", "bucket", None), P("round", "bucket", None))
 
+    line = mesh.shape["round"] == 4 and mesh.shape["bucket"] == 8
+
     def run(*arrays):
         return tuple(
             jax.shard_map(
-                body, mesh=mesh, in_specs=in_specs, out_specs=out_specs, check_vma=False
+                line_body if line else plain_body, mesh=mesh, in_specs=in_specs, out_specs=out_specs, check_vma=False
             )(*arrays)
         )
 

time: 428 us -> 243 us (0.57)
  Pallas kernels: 421 us -> 236 us
    pallas_call x1, Pallas kernels: 421 us -> 236 us  [line_body(): pl.pallas_call(functools.partial(line_kernel, names, n_r, n_b), out_shape...]
where the time goes in v1:
time: 243 us; the launch traced here: 242 us
  Pallas kernels  236 us (97%)
  local copies, waits for them, and re-layouts  5.86 us (2%)
    pallas_call x1, Pallas kernels, line_body(): pl.pallas_call(functools.partial(line_kernel, names, n_r, n_b), out_shape...  236 us
    unnamed x3, local copies, waits for them, and re-layouts  5.86 us

profile of v1, /device:TPU:0, one launch (start us, length us, event | category | flops | bytes accessed | tf_op | source)
XLA Modules:
  0.0 242.5 jit_solution(9240103231161262391)
XLA Ops:
  0.6 1.3 copy.8.refs_3_
  2.0 236.0 %shard_map.77 = (f32[1,512,512]{2,1,0:T(8,128)}, f32[1,512,512]{2,1,0:T(8,128)}) custom-call(f32[1,512,512]{2,1,0:T(8,128)} %refs_0_.1, f32[1,512,512]{2,1,0:T(8,128)} %refs_1_.1, bf16[1,512,4096]{2,1,0:T(8,128)(2,1)} %refs_2_.1, s32[1,4,3]{2,1,0:T(4,128)} %copy.8.refs_3_, f32[1,4,3,128,128]{4,3,2,1,0:T(8,128)} %refs_4_.1, s32[3,256]{1,0:T(4,128)} %refs_5_.1), custom_call_target="tpu_custom_call" | custom-call | tf_op jit(solution)/shard_map/pallas_call | solution.py:662
  237.9 2.3 copy.11
  240.2 2.3 copy.12

commit v2 on v1

--- a/solution.py
+++ b/solution.py
@@ -56,6 +56,11 @@
 
 
 def encode(value, code_ref):
+    if len(code_ref.shape) == 3:
+        wide = code_ref.shape[2]
+        for i in range(code_ref.shape[0]):
+            encode(value[:, i * wide : (i + 1) * wide], code_ref.at[i])
+        return
     rows = value.shape[0]
     top = jnp.maximum(jnp.max(jnp.abs(value), axis=0, keepdims=True), 1e-30)
     power = jnp.floor(256.0 * jnp.log2(top * (1.0 / 32767.0))) + 1.0
@@ -66,6 +71,8 @@
 
 
 def decode(code_ref):
+    if len(code_ref.shape) == 3:
+        return jnp.concatenate([decode(code_ref.at[i]) for i in range(code_ref.shape[0])], axis=1)
     rows = code_ref.shape[0] - 16
     power = code_ref[rows:, :].astype(jnp.int32).astype(jnp.float32)[0:1, :]
     unit = jnp.exp2(power * (1.0 / 256.0))
@@ -85,6 +92,8 @@
     pair = me_b // 2
     core = me_b % 2
     sibling = pair * 2 + 1 - core
+    spans = ((0, slice(0, half)), (1, slice(0, wide)), (1, slice(wide, half)))
+    quarters = (slice(0, 2), slice(2, 3), slice(3, 4))
     inner = (pair > 0) & (pair < pairs - 1)
     total_count = n_r * n_b * rows * seqs
 
@@ -174,8 +183,8 @@
 
     def set_own(s, value):
         value = value.astype(bf16)
-        for h in range(2):
-            k.blocks[me_b, h, rows_of(s), :] = value[:, h * half : (h + 1) * half]
+        for c in range(4):
+            k.blocks[me_b, c, rows_of(s), :] = value[:, c * wide : (c + 1) * wide]
 
     load_y.wait()
     for s in range(n_r):
@@ -186,27 +195,38 @@
             pl.semaphore_wait(barrier, n_b + n_r - 2)
         own_start(s)
 
+    def part_of(b, s):
+        return k.blocks.at[b, :, rows_of(s), :]
+
+    def unit_of(b, u):
+        return k.blocks.at[b, quarters[u]]
+
+    def block(b, u):
+        here = range(quarters[u].start, quarters[u].stop)
+        return jnp.concatenate([k.blocks[b, c] for c in here], axis=1)
+
     def by_parts(b):
         for s in range(n_r):
-            here = k.blocks.at[b, :, rows_of(s), :]
-            remote(here, here, k.ag_send.at[0, s], k.ag_recv.at[b, s], bucket=sibling).wait_recv()
-
-    def by_half(b, h):
-        here = k.blocks.at[b, h]
-        remote(here, here, k.ag_send.at[0, h], k.ag_recv.at[b, h], bucket=sibling).wait_recv()
-
-    def go_on(b, h, step):
-        here = k.blocks.at[b, h]
-        return remote(
-            here, here, k.line_send.at[b, h], k.ag_recv.at[b, h], bucket=me_b + step
-        )
-
-    def pass_on(b, h):
-        here = k.blocks.at[b, h]
-        return remote(here, here, k.pass_send.at[b, h], k.ag_recv.at[b, h], bucket=sibling)
-
-    def product(b, h):
-        return dot(k.pay[0, :, columns(b)], k.blocks[b, h])
+            arrived(part_of(b, s), b, s)
+
+    def by_whole(b):
+        arrived(k.blocks.at[b], b, 0)
+
+    def by_unit(b, u):
+        arrived(unit_of(b, u), b, u)
+
+    def arrived(here, b, i):
+        remote(here, here, k.ag_send.at[0, 0], k.ag_recv.at[b, i], bucket=sibling).wait_recv()
+
+    def go_on(here, b, i, step):
+        return remote(here, here, k.line_send.at[b, i], k.ag_recv.at[b, i], bucket=me_b + step)
+
+    def pass_on(here, b, i):
+        return remote(here, here, k.pass_send.at[b, i], k.ag_recv.at[b, i], bucket=sibling)
+
+    def add_product(b, u):
+        h, lanes = spans[u]
+        k.grad[h, :, lanes] += dot(k.pay[0, :, columns(b)], block(b, u))
 
     def setup():
         load_pay.wait()
@@ -239,34 +259,37 @@
         )
 
 
-    def row_copy(d, h):
+    def row_copy(d, u):
         s = (me_r + d) % n_r
         return remote(
-            k.row_q.at[s, h],
-            k.row_in.at[me_r, h],
-            k.row_send.at[s, h],
-            k.row_recv.at[me_r, h],
+            k.row_q.at[s, quarters[u]],
+            k.row_in.at[me_r, quarters[u]],
+            k.row_send.at[s, u],
+            k.row_recv.at[me_r, u],
             round=s,
         )
 
-    def row_arrival(d, h):
+    def row_arrival(d, u):
         s = (me_r + d) % n_r
-        here = k.row_in.at[s, h]
-        return remote(here, here, k.row_send.at[s, h], k.row_recv.at[s, h], round=s)
-
-    def finish(h):
+        h, lanes = spans[u]
+        here = k.row_in.at[s, quarters[u]]
+        remote(here, here, k.row_send.at[s, u], k.row_recv.at[s, u], round=s).wait_recv()
+        k.rows_f[s, h, :, lanes] = decode(here)
+
+    def finish(u):
+        h, lanes = spans[u]
         for d in range(1, n_r):
             s = (me_r + d) % n_r
-            encode(k.grad[h, rows_of(s), :], k.row_q.at[s, h])
-            row_copy(d, h).start()
-        squares = k.grad[h]
-        squares = jnp.sum((squares * squares).reshape(rows // 8, 8, half), axis=0)
-        squares = squares[:, :wide] + squares[:, wide:]
-        if h == 0:
+            encode(k.grad[h, rows_of(s), lanes], k.row_q.at[s, quarters[u]])
+            row_copy(d, u).start()
+        squares = k.grad[h, :, lanes]
+        squares = jnp.sum((squares * squares).reshape(rows // 8, 8, -1), axis=0)
+        squares = sum(squares[:, i : i + wide] for i in range(0, squares.shape[1], wide))
+        if u == 0:
             k.sq_b[me_b] = squares
         else:
             k.sq_b[me_b] += squares
-        k.rows_f[me_r, h] = k.grad[h, rows_of(me_r), :]
+        k.rows_f[me_r, h, :, lanes] = k.grad[h, rows_of(me_r), lanes]
 
     def sqb_copy(d):
         s = (me_b + d) % n_b
@@ -300,19 +323,16 @@
     def prox(sign, factor):
         for d in range(1, n_b):
             sqb_copy(d).start()
-        for d in range(1, n_r):
-            row_arrival(d, 0).wait_recv()
-            s = (me_r + d) % n_r
-            k.rows_f[s, 0] = decode(k.row_in.at[s, 0])
+        for u in range(2):
+            for d in range(1, n_r):
+                row_arrival(d, u)
         for d in range(1, n_b):
             sqb_arrival(d).wait_recv()
         k.sq_r[me_r] = jnp.sum(k.sq_b[...], axis=0)
         for d in range(1, n_r):
             sqr_copy(d).start()
         for d in range(1, n_r):
-            row_arrival(d, 1).wait_recv()
-            s = (me_r + d) % n_r
-            k.rows_f[s, 1] = decode(k.row_in.at[s, 1])
+            row_arrival(d, 2)
         for d in range(1, n_r):
             sqr_arrival(d).wait_recv()
         squares = jnp.sum(jnp.sum(k.sq_r[...], axis=0), axis=0, keepdims=True)
@@ -365,8 +385,8 @@
 
     def prox_drain():
         for d in range(1, n_r):
-            for h in range(2):
-                row_copy(d, h).wait_send()
+            for u in range(3):
+                row_copy(d, u).wait_send()
             back_copy((me_r + d) % n_r).wait_send()
             sqr_copy(d).wait_send()
         for d in range(1, n_b):
@@ -399,29 +419,36 @@
     def partial(q, h):
         return dot(k.pay_t[q, 0], k.mixed[0, h]) + dot(k.pay_t[q, 1], k.mixed[1, h])
 
-    def sum_copy(way, q, h):
+    def sum_copy(way, q, u):
         return remote(
-            k.sum_out.at[way, q, h],
-            k.sum_in.at[way, q, h],
-            k.sum_send.at[way, q, h],
-            k.sum_recv.at[way, q, h],
+            k.sum_out.at[way, q, quarters[u]],
+            k.sum_in.at[way, q, quarters[u]],
+            k.sum_send.at[way, q, u],
+            k.sum_recv.at[way, q, u],
             bucket=jnp.where(way == 0, me_b + 2, me_b - 2),
         )
 
-    def sum_arrival(way, q, h):
-        here = k.sum_in.at[way, q, h]
-        return remote(
-            here, here, k.sum_send.at[way, q, h], k.sum_recv.at[way, q, h], bucket=sibling
-        )
+    def sum_arrival(way, q, u):
+        here = k.sum_in.at[way, q, quarters[u]]
+        remote(
+            here, here, k.sum_send.at[way, q, u], k.sum_recv.at[way, q, u], bucket=sibling
+        ).wait_recv()
+        return decode(here)
 
     def sum_unit(i):
         j = i // 2
         up = (i % 2 == 0) == (pair < pairs // 2)
         way = jnp.where(up, 0, 1)
-        q = jnp.where(up, pairs - 1 - j // 2, j // 2)
+        q = jnp.where(up, pairs - 1 - j, j)
         valid = jnp.where(up, q > pair, q < pair)
         fed = jnp.where(up, pair > 0, pair < pairs - 1)
-        return way, q, j % 2, valid, fed
+        return way, q, valid, fed
+
+    def out_copy(i, s):
+        here, there = ((k.xo_ref, k.x_out), (k.yo_ref, k.y_out))[i]
+        return pltpu.make_async_copy(
+            here.at[:, rows_of(s)], there.at[:, rows_of(s)], k.out_sem.at[i, s]
+        )
 
     def step(index, _):
         weight = 2.0 / (index.astype(f32) + 3.0)
@@ -430,11 +457,17 @@
         def _():
             setup()
 
-        for h in range(2):
-            k.grad[h] = product(me_b, h)
+        outward = jnp.where(pair < pairs // 2, -2, 2)
+        first = -outward
+        second = jnp.where(inner, outward, -2 * outward)
+        far = jnp.where(inner, -2 * outward, -3 * outward)
+
+        for u in range(3):
+            h, lanes = spans[u]
+            k.grad[h, :, lanes] = dot(k.pay[0, :, columns(me_b)], block(me_b, u))
         by_parts(sibling)
-        for h in range(2):
-            k.grad[h] += product(sibling, h)
+        for u in range(2 + 1):
+            add_product(sibling, u)
 
         @pl.when(index == 0)
         def _():
@@ -443,75 +476,70 @@
             k.xo_ref[...] = (1.0 - weights[0]) * (1.0 - weights[1]) * k.xv[...]
             k.yo_ref[...] = (1.0 - weights[0]) * (1.0 - weights[1]) * k.yv[...]
 
-        def toward(place):
-            near = jnp.where(pair % 2 == 0, 2, -2)
-            side = jnp.where(pair < pairs // 2, 1, -1)
-            second = side * jnp.where(inner, 2, 4)
-            far = side * jnp.where(inner, 4, 6)
-            return (near, second, far)[place]
-
-        def take(place):
-            offset = toward(place)
-            b, other = me_b + offset, sibling + offset
-            onward = jnp.where(offset < 0, 2, -2)
-
-            def send_on(h):
-                @pl.when(inner)
-                def _():
-                    go_on(b, h, onward).start()
-
-                pass_on(b, h).start()
-
-            if place == 0:
-                by_parts(b)
-            elif place == 1:
-
-                @pl.when(inner)
-                def _():
-                    by_parts(b)
-
-            for h in range(2):
-                if place == 1:
-
-                    @pl.when(jnp.logical_not(inner))
-                    def _():
-                        by_half(b, h)
-
-                elif place == 2:
-                    by_half(b, h)
-                send_on(h)
-                if place == 2:
-                    k.grad[h] += product(b, h)
-                    by_half(other, h)
-                    k.grad[h] += product(other, h)
-                    finish(h)
-            if place < 2:
-                for h in range(2):
-                    k.grad[h] += product(b, h)
-                    by_half(other, h)
-                    k.grad[h] += product(other, h)
-
-        def take_drain(place):
-            offset = toward(place)
-            for h in range(2):
-
-                @pl.when(inner)
-                def _():
-                    go_on(me_b + offset, h, jnp.where(offset < 0, 2, -2)).wait_send()
-
-                pass_on(me_b + offset, h).wait_send()
-
-        take(0)
-
         @pl.when(index == 1)
         def _():
             for s in range(n_r):
                 add_best(k.yo_ref, s, weights[0] * (1.0 - weights[1]))
 
-        take(1)
-        take(2)
-        for place in range(3):
-            take_drain(place)
+        def both(offset):
+            for u in range(3):
+                add_product(me_b + offset, u)
+            by_whole(sibling + offset)
+            for u in range(3):
+                add_product(sibling + offset, u)
+
+        b = me_b + first
+        for s in range(n_r):
+            arrived(part_of(b, s), b, s)
+
+            @pl.when(inner)
+            def _():
+                go_on(part_of(b, s), b, s, outward).start()
+
+        pass_on(k.blocks.at[b], b, 0).start()
+        b2 = me_b + second
+
+        @pl.when(inner)
+        def _():
+            by_parts(b2)
+            for u in range(3):
+                go_on(unit_of(b2, u), b2, u, -outward).start()
+            pass_on(k.blocks.at[b2], b2, 0).start()
+
+        both(first)
+
+        @pl.when(jnp.logical_not(inner))
+        def _():
+            by_parts(b2)
+            pass_on(k.blocks.at[b2], b2, 0).start()
+
+        both(second)
+        b3 = me_b + far
+        for u in range(3):
+            by_unit(b3, u)
+
+            @pl.when(inner)
+            def _():
+                go_on(unit_of(b3, u), b3, u, outward).start()
+
+            pass_on(unit_of(b3, u), b3, u).start()
+            add_product(b3, u)
+            by_unit(sibling + far, u)
+            add_product(sibling + far, u)
+            finish(u)
+
+        @pl.when(inner)
+        def _():
+            for s in range(n_r):
+                go_on(part_of(b, s), b, s, outward).wait_send()
+            for u in range(3):
+                go_on(unit_of(b2, u), b2, u, -outward).wait_send()
+                go_on(unit_of(b3, u), b3, u, outward).wait_send()
+
+        pass_on(k.blocks.at[b], b, 0).wait_send()
+        pass_on(k.blocks.at[b2], b2, 0).wait_send()
+        for u in range(3):
+            pass_on(unit_of(b3, u), b3, u).wait_send()
         for s in range(n_r):
             own_drain(s)
 
@@ -528,54 +556,65 @@
             mixed_arrival((me_r + d) % n_r).wait_recv()
 
         def move(i, _):
-            way, q, h, valid, fed = sum_unit(i)
+            way, q, valid, fed = sum_unit(i)
 
             @pl.when(valid)
             def _():
-                k.work[...] = partial(q, h)
-
-                @pl.when(fed)
-                def _():
-                    sum_arrival(way, q, h).wait_recv()
-                    k.work[...] += decode(k.sum_in.at[way, q, h])
-
-                encode(k.work[...], k.sum_out.at[way, q, h])
-                sum_copy(way, q, h).start()
+                for u in range(3):
+                    if u != 2:
+                        k.work[...] = partial(q, min(u, 1))
+                    lanes = spans[u][1]
+
+                    @pl.when(fed)
+                    def _():
+                        k.work[:, lanes] += sum_arrival(way, q, u)
+
+                    encode(k.work[:, lanes], k.sum_out.at[way, q, quarters[u]])
+                    sum_copy(way, q, u).start()
 
             return 0
 
-        lax.fori_loop(0, 4 * (pairs - 1), move, 0)
+        lax.fori_loop(0, 2 * (pairs - 1), move, 0)
         prox_drain()
         for s in range(n_r):
             mixed_copy(s).wait_send()
         share = jnp.where(index == 0, weights[0] * (1.0 - weights[1]), weights[1])
         for s in range(n_r):
             add_best(k.xo_ref, s, share)
+
+            @pl.when(index == 1)
+            def _():
+                out_copy(0, s).start()
+
         for h in range(2):
             k.grad[h] = partial(pair, h)
+        for u in range(3):
+            h, lanes = spans[u]
+
+            def add_sum(way):
+                k.grad[h, :, lanes] += sum_arrival(way, pair, u)
 
             @pl.when(pair > 0)
             def _():
-                sum_arrival(0, pair, h).wait_recv()
-                k.grad[h] += decode(k.sum_in.at[0, pair, h])
+                add_sum(0)
 
             @pl.when(pair < pairs - 1)
             def _():
-                sum_arrival(1, pair, h).wait_recv()
-                k.grad[h] += decode(k.sum_in.at[1, pair, h])
-
-            finish(h)
+                add_sum(1)
+
+            finish(u)
 
         def settle(i, _):
-            way, q, h, valid, fed = sum_unit(i)
+            way, q, valid, fed = sum_unit(i)
 
             @pl.when(valid)
             def _():
-                sum_copy(way, q, h).wait_send()
+                for u in range(3):
+                    sum_copy(way, q, u).wait_send()
 
             return 0
 
-        lax.fori_loop(0, 4 * (pairs - 1), settle, 0)
+        lax.fori_loop(0, 2 * (pairs - 1), settle, 0)
 
         prox(1.0, smooth_y)
         for d in range(n_r):
@@ -591,11 +630,20 @@
             @pl.when(index == 1)
             def _():
                 add_best(k.yo_ref, s, weights[1])
+                out_copy(1, s).start()
 
         prox_drain()
         return 0
 
     lax.fori_loop(0, 2, step, 0)
+    for i in range(2):
+        for s in range(n_r):
+            out_copy(i, s).wait()
+
+
+def place_kernel(x_in, y_in, x_out, y_out):
+    x_out[...] = x_in[...]
+    y_out[...] = y_in[...]
 
 
 def line_body(x_start, y_start, bucket_payoff, column_blocks, public_coef, predecessor_sequences):
@@ -613,10 +661,12 @@
     scratch = dict(
         xv=pltpu.VMEM((1, rows, seqs), f32),
         yv=pltpu.VMEM((1, rows, seqs), f32),
+        xo_ref=pltpu.VMEM((1, rows, seqs), f32),
+        yo_ref=pltpu.VMEM((1, rows, seqs), f32),
         pay=pltpu.VMEM((1, rows, n_b * rows), bf16),
         pay_t=pltpu.VMEM((pairs, 2, rows, rows), bf16),
         pay_out=pltpu.VMEM((pairs, rows, rows), bf16),
-        blocks=pltpu.VMEM((n_b, 2, rows, half), bf16),
+        blocks=pltpu.VMEM((n_b, 4, rows, half // 2), bf16),
         mixed=pltpu.VMEM((2, 2, rows, half), bf16),
         mixer=pltpu.VMEM((seqs, seqs), f32),
         mix_p=pltpu.VMEM((3, seqs, seqs), bf16),
@@ -627,10 +677,10 @@
         f_y=pltpu.VMEM((rows, seqs), f32),
         grad=pltpu.VMEM((2, rows, half), f32),
         work=pltpu.VMEM((rows, half), f32),
-        sum_out=pltpu.VMEM((2, pairs, 2, rows + 16, half), i16),
-        sum_in=pltpu.VMEM((2, pairs, 2, rows + 16, half), i16),
-        row_q=pltpu.VMEM((n_r, 2, part + 16, half), i16),
-        row_in=pltpu.VMEM((n_r, 2, part + 16, half), i16),
+        sum_out=pltpu.VMEM((2, pairs, 4, rows + 16, half // 2), i16),
+        sum_in=pltpu.VMEM((2, pairs, 4, rows + 16, half // 2), i16),
+        row_q=pltpu.VMEM((n_r, 4, part + 16, half // 2), i16),
+        row_in=pltpu.VMEM((n_r, 4, part + 16, half // 2), i16),
         rows_f=pltpu.VMEM((n_r, 2, part, half), f32),
         share=pltpu.VMEM((n_r, 2, part, half), f32),
         back_q=pltpu.VMEM((n_r, part, seqs), i16),
@@ -638,18 +688,19 @@
         sq_b=pltpu.VMEM((n_b, 8, 128), f32),
         sq_r=pltpu.VMEM((n_r, 8, 128), f32),
         load_sem=dma((3,)),
+        out_sem=dma((2, n_r)),
         turn_send=dma((pairs,)),
         turn_recv=dma((pairs,)),
         ag_send=dma((3, n_r)),
         ag_recv=dma((n_b, n_r)),
-        line_send=dma((n_b, 2)),
-        pass_send=dma((n_b, 2)),
+        line_send=dma((n_b, n_r)),
+        pass_send=dma((n_b, 3)),
         mx_send=dma((n_r,)),
         mx_recv=dma((2, n_r)),
-        sum_send=dma((2, pairs, 2)),
-        sum_recv=dma((2, pairs, 2)),
-        row_send=dma((n_r, 2)),
-        row_recv=dma((n_r, 2)),
+        sum_send=dma((2, pairs, 3)),
+        sum_recv=dma((2, pairs, 3)),
+        row_send=dma((n_r, 3)),
+        row_recv=dma((n_r, 3)),
         back_send=dma((n_r,)),
         back_recv=dma((n_r,)),
         sqb_send=dma((n_b,)),
@@ -657,18 +708,26 @@
         sqr_send=dma((n_r,)),
         sqr_recv=dma((n_r,)),
     )
-    names = ["x_hbm", "y_hbm", "pay_hbm", "col_ref", "coef_ref", "pred_ref", "xo_ref", "yo_ref"]
+    names = ["x_hbm", "y_hbm", "pay_hbm", "col_ref", "coef_ref", "pred_ref", "x_out", "y_out"]
     names += list(scratch)
-    return pl.pallas_call(
+    found = pl.pallas_call(
         functools.partial(line_kernel, names, n_r, n_b),
         out_shape=[jax.ShapeDtypeStruct(x_start.shape, f32)] * 2,
         in_specs=[hbm, hbm, hbm, smem, vmem, vmem],
-        out_specs=[vmem, vmem],
+        out_specs=[hbm, hbm],
         scratch_shapes=list(scratch.values()),
         compiler_params=pltpu.CompilerParams(
             collective_id=0, has_side_effects=True, vmem_limit_bytes=60 * 1024 * 1024
         ),
     )(x_start, y_start, bucket_payoff, column_blocks, public_coef, predecessor_sequences)
+    block = pl.BlockSpec((1, rows // 2, seqs), lambda i: (0, i, 0))
+    return pl.pallas_call(
+        place_kernel,
+        grid=(2,),
+        out_shape=[jax.ShapeDtypeStruct(x_start.shape, f32)] * 2,
+        in_specs=[block, block],
+        out_specs=[block, block],
+    )(*found)
 
 
 def plain_kernel(

time: 243 us -> 224 us (0.922)
  Pallas kernels: 236 us -> 222 us
  local copies, waits for them, and re-layouts: 5.86 us -> 1.34 us
    pallas_call x1, Pallas kernels: 236 us -> 220 us  [line_body(): pl.pallas_call(functools.partial(line_kernel, names, n_r, n_b), out_shape...]
    unnamed x3 -> x1, local copies, waits for them, and re-layouts: 5.86 us -> 1.34 us
    pallas_call x0 -> x1, Pallas kernels: none -> 2.59 us  [line_body(): pl.pallas_call(place_kernel, grid=(2,), out_shape=[jax.ShapeDtypeStruct(x...]
where the time goes in v2:
time: 224 us
  Pallas kernels  222 us (99%)
    pallas_call x1, Pallas kernels, line_body(): pl.pallas_call(functools.partial(line_kernel, names, n_r, n_b), out_shape...  220 us

profile of v2, /device:TPU:0, one launch (start us, length us, event | category | flops | bytes accessed | tf_op | source)
XLA Modules:
  0.0 224.3 jit_solution(3269880272892144086)
XLA Ops:
  0.6 1.3 copy.8.refs_3_
  2.0 219.7 %shard_map.77 = (f32[1,512,512]{2,1,0:T(8,128)}, f32[1,512,512]{2,1,0:T(8,128)}) custom-call(f32[1,512,512]{2,1,0:T(8,128)} %refs_0_.1, f32[1,512,512]{2,1,0:T(8,128)} %refs_1_.1, bf16[1,512,4096]{2,1,0:T(8,128)(2,1)} %refs_2_.1, s32[1,4,3]{2,1,0:T(4,128)} %copy.8.refs_3_, f32[1,4,3,128,128]{4,3,2,1,0:T(8,128)} %refs_4_.1, s32[3,256]{1,0:T(4,128)} %refs_5_.1), custom_call_target="tpu_custom_call" | custom-call | tf_op jit(solution)/shard_map/pallas_call | solution.py:713
  221.7 2.6 %shard_map.78 = (f32[1,512,512]{2,1,0:T(8,128)}, f32[1,512,512]{2,1,0:T(8,128)}) custom-call(f32[1,512,512]{2,1,0:T(8,128)} %get-tuple-element.4.x_in, f32[1,512,512]{2,1,0:T(8,128)} %get-tuple-element.5.y_in), custom_call_target="tpu_custom_call" | custom-call | tf_op jit(solution)/shard_map/pallas_call | solution.py:724

commit v3 on v2

--- a/solution.py
+++ b/solution.py
@@ -94,6 +94,11 @@
     sibling = pair * 2 + 1 - core
     spans = ((0, slice(0, half)), (1, slice(0, wide)), (1, slice(wide, half)))
     quarters = (slice(0, 2), slice(2, 3), slice(3, 4))
+    members = ((0, 1), (2,), (3,))
+    outward = jnp.where(pair < pairs // 2, -2, 2)
+    end_chip = jnp.where(pair < pairs // 2, 0, pairs - 1)
+    facing = pair - outward // 2
+    far_end = pairs - 1 - end_chip
     inner = (pair > 0) & (pair < pairs - 1)
     total_count = n_r * n_b * rows * seqs
 
@@ -153,6 +158,52 @@
     def columns(j):
         return pl.ds(pl.multiple_of(j * rows, rows), rows)
 
+    away = jnp.where(pair < pairs // 2, pairs // 2, 0)
+
+    def lent_place(o):
+        return (far_end - away, 1 - (far_end - away))[o]
+
+    def lend(turn):
+        o, i, p = turn // 4, turn // 2 % 2, turn % 2
+        here = pl.ds(p * (rows // 2), rows // 2)
+        b = 2 * lent_place(o) + i
+        return remote(
+            k.pay.at[0, here, columns(2 * away + b)],
+            k.lent.at[b, here],
+            k.lend_send.at[turn],
+            k.lend_recv.at[turn],
+            bucket=me_b - outward,
+        )
+
+    def lend_start(turns):
+        @pl.when(jnp.logical_not(inner))
+        def _():
+            for turn in turns:
+                lend(turn).start()
+
+    def lent_swap(j, o):
+        return remote(
+            k.pay_out.at[j],
+            k.lent_t.at[j, core],
+            k.swap_send.at[o],
+            k.swap_recv.at[o],
+            bucket=sibling,
+        )
+
+    def take_lent(o):
+        j = lent_place(o)
+        for i in range(2):
+            for p in range(2):
+                here = k.lent.at[2 * j + i, pl.ds(p * (rows // 2), rows // 2)]
+                turn = 4 * o + 2 * i + p
+                remote(
+                    here, here, k.lend_send.at[turn], k.lend_recv.at[turn], bucket=sibling
+                ).wait_recv()
+        k.pay_out[j] = k.lent[2 * j + 1 - core].T
+        lent_swap(j, o).start()
+        k.lent_t[j, core] = k.lent[2 * j + core].T
+        lent_swap(j, o).wait()
+
 
     def own_copy(kind, s):
         target = (sibling, me_b + 2, me_b - 2)[kind]
@@ -186,24 +237,24 @@
         for c in range(4):
             k.blocks[me_b, c, rows_of(s), :] = value[:, c * wide : (c + 1) * wide]
 
+    pl.semaphore_wait(barrier, n_b + n_r - 2)
     load_y.wait()
+    load_pay.wait()
+    lend_start(range(1))
     for s in range(n_r):
         value = mix(split3(k.yv[0, rows_of(s), :]), [k.mix_p[i] for i in range(3)], nt)
         k.f_y[rows_of(s), :] = value
         set_own(s, value)
-        if s == 0:
-            pl.semaphore_wait(barrier, n_b + n_r - 2)
         own_start(s)
 
     def part_of(b, s):
         return k.blocks.at[b, :, rows_of(s), :]
 
-    def unit_of(b, u):
-        return k.blocks.at[b, quarters[u]]
+    def unit_of(b, c):
+        return k.blocks.at[b, c]
 
     def block(b, u):
-        here = range(quarters[u].start, quarters[u].stop)
-        return jnp.concatenate([k.blocks[b, c] for c in here], axis=1)
+        return jnp.concatenate([k.blocks[b, c] for c in members[u]], axis=1)
 
     def by_parts(b):
         for s in range(n_r):
@@ -212,8 +263,8 @@
     def by_whole(b):
         arrived(k.blocks.at[b], b, 0)
 
-    def by_unit(b, u):
-        arrived(unit_of(b, u), b, u)
+    def by_unit(b, c):
+        arrived(unit_of(b, c), b, c)
 
     def arrived(here, b, i):
         remote(here, here, k.ag_send.at[0, 0], k.ag_recv.at[b, i], bucket=sibling).wait_recv()
@@ -225,11 +276,16 @@
         return remote(here, here, k.pass_send.at[b, i], k.ag_recv.at[b, i], bucket=sibling)
 
     def add_product(b, u):
-        h, lanes = spans[u]
-        k.grad[h, :, lanes] += dot(k.pay[0, :, columns(b)], block(b, u))
+        value = dot(k.pay[0, :, columns(b)], block(b, u))
+        for i, c in enumerate(members[u]):
+            k.grad[c] += value[:, i * wide : (i + 1) * wide]
+
+    def lent_product(b, c):
+        return dot(k.lent[b - 2 * away], k.blocks[b, c])
 
     def setup():
-        load_pay.wait()
+        lend_start(range(1, 5))
+
 
         def turn(q, _):
             k.pay_out[q] = k.pay[0, :, columns(q * 2 + 1 - core)].T
@@ -277,19 +333,20 @@
         k.rows_f[s, h, :, lanes] = decode(here)
 
     def finish(u):
-        h, lanes = spans[u]
         for d in range(1, n_r):
             s = (me_r + d) % n_r
-            encode(k.grad[h, rows_of(s), lanes], k.row_q.at[s, quarters[u]])
+            for c in members[u]:
+                encode(k.grad[c, rows_of(s), :], k.row_q.at[s, c])
             row_copy(d, u).start()
-        squares = k.grad[h, :, lanes]
-        squares = jnp.sum((squares * squares).reshape(rows // 8, 8, -1), axis=0)
-        squares = sum(squares[:, i : i + wide] for i in range(0, squares.shape[1], wide))
-        if u == 0:
-            k.sq_b[me_b] = squares
-        else:
-            k.sq_b[me_b] += squares
-        k.rows_f[me_r, h, :, lanes] = k.grad[h, rows_of(me_r), lanes]
+        for c in members[u]:
+            squares = k.grad[c]
+            squares = jnp.sum((squares * squares).reshape(rows // 8, 8, wide), axis=0)
+            if c == 0:
+                k.sq_b[me_b] = squares
+            else:
+                k.sq_b[me_b] += squares
+            h, lanes = c // 2, slice(c % 2 * wide, c % 2 * wide + wide)
+            k.rows_f[me_r, h, :, lanes] = k.grad[c, rows_of(me_r), :]
 
     def sqb_copy(d):
         s = (me_b + d) % n_b
@@ -320,7 +377,7 @@
         here = k.back_in.at[s]
         return remote(here, here, k.back_send.at[s], k.back_recv.at[s], round=s)
 
-    def prox(sign, factor):
+    def prox(sign, factor, after_scale=None):
         for d in range(1, n_b):
             sqb_copy(d).start()
         for u in range(2):
@@ -339,6 +396,8 @@
         squares = jnp.sum(squares, axis=1, keepdims=True)
         scale = sign / (factor * jnp.sqrt(squares / total_count + epsilon))
 
+        if after_scale is not None:
+            after_scale()
         carried = None
         shares = [None] * n_r
         for r in reversed(range(n_r)):
@@ -416,33 +475,125 @@
         here = k.mixed.at[1 - core, :, rows_of(s), :]
         return remote(here, here, k.mx_send.at[s], k.mx_recv.at[1 - core, s], bucket=sibling)
 
-    def partial(q, h):
-        return dot(k.pay_t[q, 0], k.mixed[0, h]) + dot(k.pay_t[q, 1], k.mixed[1, h])
-
-    def sum_copy(way, q, u):
+    def raw_copy(n):
         return remote(
-            k.sum_out.at[way, q, quarters[u]],
-            k.sum_in.at[way, q, quarters[u]],
-            k.sum_send.at[way, q, u],
-            k.sum_recv.at[way, q, u],
-            bucket=jnp.where(way == 0, me_b + 2, me_b - 2),
+            k.mixed.at[core, n],
+            k.mixed.at[2 + core, n],
+            k.raw_send.at[n],
+            k.raw_recv.at[core, n],
+            bucket=me_b - outward,
         )
 
-    def sum_arrival(way, q, u):
-        here = k.sum_in.at[way, q, quarters[u]]
+    def raw_pass(n):
+        here = k.mixed.at[2 + core, n]
+        return remote(here, here, k.raw_send.at[n], k.raw_recv.at[core, n], bucket=sibling)
+
+    def raw_arrival(source, n):
+        here = k.mixed.at[2 + source, n]
         remote(
-            here, here, k.sum_send.at[way, q, u], k.sum_recv.at[way, q, u], bucket=sibling
+            here, here, k.raw_send.at[n], k.raw_recv.at[source, n], bucket=sibling
+        ).wait_recv()
+
+    def partial(q, n):
+        return dot(k.pay_t[q, 0], k.mixed[0, n]) + dot(k.pay_t[q, 1], k.mixed[1, n])
+
+    def lent_partial(j, n):
+        return dot(k.lent_t[j, 0], k.mixed[2, n]) + dot(k.lent_t[j, 1], k.mixed[3, n])
+
+    def sum_copy(kind, n, step):
+        return remote(
+            k.sum_out.at[kind, n],
+            k.sum_in.at[kind, n],
+            k.sum_send.at[kind, n],
+            k.sum_recv.at[kind, n],
+            bucket=me_b + step,
+        )
+
+    def sum_arrival(kind, n):
+        here = k.sum_in.at[kind, n]
+        remote(
+            here, here, k.sum_send.at[kind, n], k.sum_recv.at[kind, n], bucket=sibling
         ).wait_recv()
         return decode(here)
 
-    def sum_unit(i):
-        j = i // 2
-        up = (i % 2 == 0) == (pair < pairs // 2)
-        way = jnp.where(up, 0, 1)
-        q = jnp.where(up, pairs - 1 - j, j)
-        valid = jnp.where(up, q > pair, q < pair)
-        fed = jnp.where(up, pair > 0, pair < pairs - 1)
-        return way, q, valid, fed
+    def sums_of_end(index):
+        for n in range(4):
+            raw_copy(n).start()
+
+        def lend_sum(n, _):
+            k.work[...] = partial(facing - outward // 2, n)
+            encode(k.work[...], k.sum_out.at[4, n])
+            sum_copy(4, n, -outward).start()
+            return 0
+
+        @pl.when(index == 0)
+        def _():
+            lax.fori_loop(0, 4, lend_sum, 0)
+
+        def give(n, _):
+            k.work[...] = partial(facing, n)
+            encode(k.work[...], k.sum_out.at[3, n])
+            sum_copy(3, n, -outward).start()
+            return 0
+
+        lax.fori_loop(0, 4, give, 0)
+
+    def sums_of_inner(index):
+        def give(i, _):
+            n = i % 4
+
+            @pl.when(i < 4)
+            def _():
+                raw_arrival(core, n)
+                raw_pass(n).start()
+
+            q = jnp.where(i < 4, far_end, facing)
+            k.work[...] = partial(q, n)
+
+            @pl.when(i < 4)
+            def _():
+                raw_arrival(1 - core, n)
+
+            @pl.when((i < 4) | (index == 1))
+            def _():
+                k.work[...] += lent_partial(q - away, n)
+
+            @pl.when((i >= 4) & (index == 0))
+            def _():
+                k.work[...] += sum_arrival(4, n)
+
+            encode(k.work[...], k.sum_out.at[i // 4, n])
+            sum_copy(i // 4, n, -outward).start()
+
+            @pl.when((i >= 2) & (i < 6))
+            def _():
+                k.work[...] = partial(end_chip, i - 2)
+                k.work[...] += sum_arrival(0, i - 2)
+                encode(k.work[...], k.sum_out.at[2, i - 2])
+                sum_copy(2, i - 2, outward).start()
+
+            return 0
+
+        lax.fori_loop(0, 8, give, 0)
+
+    def sums_drain(index):
+        @pl.when(inner)
+        def _():
+            for n in range(4):
+                raw_pass(n).wait_send()
+                sum_copy(0, n, -outward).wait_send()
+                sum_copy(1, n, -outward).wait_send()
+                sum_copy(2, n, outward).wait_send()
+
+        @pl.when(jnp.logical_not(inner))
+        def _():
+            for n in range(4):
+                raw_copy(n).wait_send()
+                sum_copy(3, n, -outward).wait_send()
+
+                @pl.when(index == 0)
+                def _():
+                    sum_copy(4, n, -outward).wait_send()
 
     def out_copy(i, s):
         here, there = ((k.xo_ref, k.x_out), (k.yo_ref, k.y_out))[i]
@@ -457,14 +608,14 @@
         def _():
             setup()
 
-        outward = jnp.where(pair < pairs // 2, -2, 2)
         first = -outward
         second = jnp.where(inner, outward, -2 * outward)
         far = jnp.where(inner, -2 * outward, -3 * outward)
 
         for u in range(3):
-            h, lanes = spans[u]
-            k.grad[h, :, lanes] = dot(k.pay[0, :, columns(me_b)], block(me_b, u))
+            value = dot(k.pay[0, :, columns(me_b)], block(me_b, u))
+            for i, c in enumerate(members[u]):
+                k.grad[c] = value[:, i * wide : (i + 1) * wide]
         by_parts(sibling)
         for u in range(2 + 1):
             add_product(sibling, u)
@@ -488,11 +639,12 @@
             for u in range(3):
                 add_product(sibling + offset, u)
 
+        plain = index == 0
         b = me_b + first
         for s in range(n_r):
             arrived(part_of(b, s), b, s)
 
-            @pl.when(inner)
+            @pl.when(inner & plain)
             def _():
                 go_on(part_of(b, s), b, s, outward).start()
 
@@ -502,79 +654,123 @@
         @pl.when(inner)
         def _():
             by_parts(b2)
-            for u in range(3):
-                go_on(unit_of(b2, u), b2, u, -outward).start()
+            for c in range(4):
+                go_on(unit_of(b2, c), b2, c, -outward).start()
             pass_on(k.blocks.at[b2], b2, 0).start()
 
         both(first)
 
-        @pl.when(jnp.logical_not(inner))
+        @pl.when(jnp.logical_not(inner) & plain)
         def _():
             by_parts(b2)
             pass_on(k.blocks.at[b2], b2, 0).start()
 
-        both(second)
+        @pl.when(inner | plain)
+        def _():
+            both(second)
+
+        @pl.when(inner & jnp.logical_not(plain))
+        def _():
+            take_lent(1)
+            for c in range(4):
+                k.early[c] = lent_product(b, c) + lent_product(sibling + first, c)
+
         b3 = me_b + far
-        for u in range(3):
-            by_unit(b3, u)
-
-            @pl.when(inner)
-            def _():
-                go_on(unit_of(b3, u), b3, u, outward).start()
-
-            pass_on(unit_of(b3, u), b3, u).start()
-            add_product(b3, u)
-            by_unit(sibling + far, u)
-            add_product(sibling + far, u)
-            finish(u)
+        for c in range(4):
+
+            @pl.when(inner | plain)
+            def _():
+                by_unit(b3, c)
+
+                @pl.when(inner & plain)
+                def _():
+                    go_on(unit_of(b3, c), b3, c, outward).start()
+
+                pass_on(unit_of(b3, c), b3, c).start()
+
+                @pl.when(plain)
+                def _():
+                    k.grad[c] += dot(k.pay[0, :, columns(b3)], k.blocks[b3, c])
+
+                by_unit(sibling + far, c)
+
+                @pl.when(jnp.logical_not(plain))
+                def _():
+                    k.early[c] += lent_product(b3, c) + lent_product(sibling + far, c)
+                    encode(k.early[c], k.sum_out.at[5, c])
+                    sum_copy(5, c, outward).start()
+                    k.grad[c] += dot(k.pay[0, :, columns(b3)], k.blocks[b3, c])
+
+                k.grad[c] += dot(k.pay[0, :, columns(sibling + far)], k.blocks[sibling + far, c])
+
+            @pl.when(jnp.logical_not(inner | plain))
+            def _():
+                k.grad[c] += sum_arrival(5, c)
+
+            if c > 0:
+                finish(c - 1)
+
+        @pl.when(inner & plain)
+        def _():
+            for c in range(4):
+                go_on(part_of(b, c), b, c, outward).wait_send()
+                go_on(unit_of(b3, c), b3, c, outward).wait_send()
 
         @pl.when(inner)
         def _():
-            for s in range(n_r):
-                go_on(part_of(b, s), b, s, outward).wait_send()
-            for u in range(3):
-                go_on(unit_of(b2, u), b2, u, -outward).wait_send()
-                go_on(unit_of(b3, u), b3, u, outward).wait_send()
+            for c in range(4):
+                go_on(unit_of(b2, c), b2, c, -outward).wait_send()
 
         pass_on(k.blocks.at[b], b, 0).wait_send()
-        pass_on(k.blocks.at[b2], b2, 0).wait_send()
-        for u in range(3):
-            pass_on(unit_of(b3, u), b3, u).wait_send()
+
+        @pl.when(inner | plain)
+        def _():
+            pass_on(k.blocks.at[b2], b2, 0).wait_send()
+            for c in range(4):
+                pass_on(unit_of(b3, c), b3, c).wait_send()
+
+        @pl.when(inner & jnp.logical_not(plain))
+        def _():
+            for c in range(4):
+                sum_copy(5, c, outward).wait_send()
+
+        @pl.when(jnp.logical_not(inner | plain))
+        def _():
+            for turn in range(8):
+                lend(turn).wait_send()
+
         for s in range(n_r):
             own_drain(s)
 
-        prox(-1.0, smooth_x)
+        def lend_more(turns):
+            @pl.when(index == 0)
+            def _():
+                lend_start(turns)
+
+        prox(-1.0, smooth_x, functools.partial(lend_more, range(5, 7)))
         for d in range(n_r):
             s = (me_r + d) % n_r
             if d > 0:
                 back_arrival(s).wait_recv()
             value = mixed_part(s, k.f_x, weight, nn).astype(bf16)
-            for h in range(2):
-                k.mixed[core, h, rows_of(s), :] = value[:, h * half : (h + 1) * half]
+            for c in range(4):
+                k.mixed[core, c, rows_of(s), :] = value[:, c * wide : (c + 1) * wide]
             mixed_copy(s).start()
         for d in range(n_r):
             mixed_arrival((me_r + d) % n_r).wait_recv()
 
-        def move(i, _):
-            way, q, valid, fed = sum_unit(i)
-
-            @pl.when(valid)
-            def _():
-                for u in range(3):
-                    if u != 2:
-                        k.work[...] = partial(q, min(u, 1))
-                    lanes = spans[u][1]
-
-                    @pl.when(fed)
-                    def _():
-                        k.work[:, lanes] += sum_arrival(way, q, u)
-
-                    encode(k.work[:, lanes], k.sum_out.at[way, q, quarters[u]])
-                    sum_copy(way, q, u).start()
-
-            return 0
-
-        lax.fori_loop(0, 2 * (pairs - 1), move, 0)
+        @pl.when(inner)
+        def _():
+            @pl.when(index == 0)
+            def _():
+                take_lent(0)
+
+            sums_of_inner(index)
+
+        @pl.when(jnp.logical_not(inner))
+        def _():
+            sums_of_end(index)
+
         prox_drain()
         for s in range(n_r):
             mixed_copy(s).wait_send()
@@ -586,37 +782,24 @@
             def _():
                 out_copy(0, s).start()
 
-        for h in range(2):
-            k.grad[h] = partial(pair, h)
+        for n in range(4):
+            k.grad[n] = partial(pair, n)
         for u in range(3):
-            h, lanes = spans[u]
-
-            def add_sum(way):
-                k.grad[h, :, lanes] += sum_arrival(way, pair, u)
-
-            @pl.when(pair > 0)
-            def _():
-                add_sum(0)
-
-            @pl.when(pair < pairs - 1)
-            def _():
-                add_sum(1)
+            for n in members[u]:
+
+                @pl.when(inner)
+                def _():
+                    k.grad[n] += sum_arrival(3, n)
+                    k.grad[n] += sum_arrival(1, n)
+
+                @pl.when(jnp.logical_not(inner))
+                def _():
+                    k.grad[n] += sum_arrival(2, n)
 
             finish(u)
-
-        def settle(i, _):
-            way, q, valid, fed = sum_unit(i)
-
-            @pl.when(valid)
-            def _():
-                for u in range(3):
-                    sum_copy(way, q, u).wait_send()
-
-            return 0
-
-        lax.fori_loop(0, 2 * (pairs - 1), settle, 0)
-
-        prox(1.0, smooth_y)
+        sums_drain(index)
+
+        prox(1.0, smooth_y, functools.partial(lend_more, range(7, 8)))
         for d in range(n_r):
             s = (me_r + d) % n_r
             if d > 0:
@@ -667,7 +850,7 @@
         pay_t=pltpu.VMEM((pairs, 2, rows, rows), bf16),
         pay_out=pltpu.VMEM((pairs, rows, rows), bf16),
         blocks=pltpu.VMEM((n_b, 4, rows, half // 2), bf16),
-        mixed=pltpu.VMEM((2, 2, rows, half), bf16),
+        mixed=pltpu.VMEM((4, 4, rows, half // 2), bf16),
         mixer=pltpu.VMEM((seqs, seqs), f32),
         mix_p=pltpu.VMEM((3, seqs, seqs), bf16),
         to_outer=pltpu.VMEM((seqs, seqs), bf16),
@@ -675,10 +858,13 @@
         spread=pltpu.VMEM((n_r - 1, half, seqs), bf16),
         f_x=pltpu.VMEM((rows, seqs), f32),
         f_y=pltpu.VMEM((rows, seqs), f32),
-        grad=pltpu.VMEM((2, rows, half), f32),
-        work=pltpu.VMEM((rows, half), f32),
-        sum_out=pltpu.VMEM((2, pairs, 4, rows + 16, half // 2), i16),
-        sum_in=pltpu.VMEM((2, pairs, 4, rows + 16, half // 2), i16),
+        grad=pltpu.VMEM((4, rows, half // 2), f32),
+        work=pltpu.VMEM((rows, half // 2), f32),
+        early=pltpu.VMEM((4, rows, half // 2), f32),
+        lent=pltpu.VMEM((4, rows, rows), bf16),
+        lent_t=pltpu.VMEM((2, 2, rows, rows), bf16),
+        sum_out=pltpu.VMEM((6, 4, rows + 16, half // 2), i16),
+        sum_in=pltpu.VMEM((6, 4, rows + 16, half // 2), i16),
         row_q=pltpu.VMEM((n_r, 4, part + 16, half // 2), i16),
         row_in=pltpu.VMEM((n_r, 4, part + 16, half // 2), i16),
         rows_f=pltpu.VMEM((n_r, 2, part, half), f32),
@@ -694,11 +880,17 @@
         ag_send=dma((3, n_r)),
         ag_recv=dma((n_b, n_r)),
         line_send=dma((n_b, n_r)),
-        pass_send=dma((n_b, 3)),
+        pass_send=dma((n_b, 4)),
         mx_send=dma((n_r,)),
         mx_recv=dma((2, n_r)),
-        sum_send=dma((2, pairs, 3)),
-        sum_recv=dma((2, pairs, 3)),
+        sum_send=dma((6, 4)),
+        sum_recv=dma((6, 4)),
+        lend_send=dma((8,)),
+        lend_recv=dma((8,)),
+        swap_send=dma((2,)),
+        swap_recv=dma((2,)),
+        raw_send=dma((4,)),
+        raw_recv=dma((2, 4)),
         row_send=dma((n_r, 3)),
         row_recv=dma((n_r, 3)),
         back_send=dma((n_r,)),

time: 224 us -> 220 us (0.982)
  Pallas kernels: 222 us -> 218 us
    pallas_call x1, Pallas kernels: 220 us -> 215 us  [line_body(): pl.pallas_call(functools.partial(line_kernel, names, n_r, n_b), out_shape...]
where the time goes in v3:
time: 220 us; the launch traced here: 219 us
  Pallas kernels  218 us (99%)
    pallas_call x1, Pallas kernels, line_body(): pl.pallas_call(functools.partial(line_kernel, names, n_r, n_b), out_shape...  215 us

profile of v3, /device:TPU:0, one launch (start us, length us, event | category | flops | bytes accessed | tf_op | source)
XLA Modules:
  0.0 219.5 jit_solution(9464972603797816591)
XLA Ops:
  0.6 1.3 copy.8.refs_3_
  2.0 214.9 %shard_map.77 = (f32[1,512,512]{2,1,0:T(8,128)}, f32[1,512,512]{2,1,0:T(8,128)}) custom-call(f32[1,512,512]{2,1,0:T(8,128)} %refs_0_.1, f32[1,512,512]{2,1,0:T(8,128)} %refs_1_.1, bf16[1,512,4096]{2,1,0:T(8,128)(2,1)} %refs_2_.1, s32[1,4,3]{2,1,0:T(4,128)} %copy.8.refs_3_, f32[1,4,3,128,128]{4,3,2,1,0:T(8,128)} %refs_4_.1, s32[3,256]{1,0:T(4,128)} %refs_5_.1), custom_call_target="tpu_custom_call" | custom-call | tf_op jit(solution)/shard_map/pallas_call | solution.py:905
  216.9 2.6 %shard_map.78 = (f32[1,512,512]{2,1,0:T(8,128)}, f32[1,512,512]{2,1,0:T(8,128)}) custom-call(f32[1,512,512]{2,1,0:T(8,128)} %get-tuple-element.4.x_in, f32[1,512,512]{2,1,0:T(8,128)} %get-tuple-element.5.y_in), custom_call_target="tpu_custom_call" | custom-call | tf_op jit(solution)/shard_map/pallas_call | solution.py:916

commit v4 on v3

--- a/solution.py
+++ b/solution.py
@@ -120,20 +120,15 @@
     load_x.start()
 
     barrier = pltpu.get_barrier_semaphore()
-    for d in range(1, n_b):
-        pl.semaphore_signal(
-            barrier,
-            inc=1,
-            device_id={"bucket": (me_b + d) % n_b},
-            device_id_type=pl.DeviceIdType.MESH,
-        )
-    for d in range(1, n_r):
-        pl.semaphore_signal(
-            barrier,
-            inc=1,
-            device_id={"round": (me_r + d) % n_r},
-            device_id_type=pl.DeviceIdType.MESH,
-        )
+    for dr in range(n_r):
+        for db in range(n_b):
+            if dr or db:
+                pl.semaphore_signal(
+                    barrier,
+                    inc=1,
+                    device_id={"round": (me_r + dr) % n_r, "bucket": (me_b + db) % n_b},
+                    device_id_type=pl.DeviceIdType.MESH,
+                )
 
     def order(i):
         return 2 * (i // half * wide + i % wide) + (i % half) // wide
@@ -237,7 +232,7 @@
         for c in range(4):
             k.blocks[me_b, c, rows_of(s), :] = value[:, c * wide : (c + 1) * wide]
 
-    pl.semaphore_wait(barrier, n_b + n_r - 2)
+    pl.semaphore_wait(barrier, n_b * n_r - 1)
     load_y.wait()
     load_pay.wait()
     lend_start(range(1))
@@ -299,6 +294,14 @@
             one_hot = (place == k.pred_ref[r : r + 1, :]).astype(f32).astype(bf16)
             k.gather[r] = one_hot
             k.spread[r] = one_hot.T
+
+        @pl.when(me_r == 0)
+        def _():
+            for s in range(n_r):
+                k.back_in[s, 1] = jnp.full((part, half), 65535 - shift_code, jnp.int32).astype(
+                    jnp.int16
+                )
+
         load_x.wait()
         value = picked(split3(exact(k.xv[0], k.mixer[...])), k.to_outer[...], nt)
         k.f_x[...] = value
@@ -342,67 +345,95 @@
             squares = k.grad[c]
             squares = jnp.sum((squares * squares).reshape(rows // 8, 8, wide), axis=0)
             if c == 0:
-                k.sq_b[me_b] = squares
+                k.sq_mine[...] = squares
             else:
-                k.sq_b[me_b] += squares
+                k.sq_mine[...] += squares
             h, lanes = c // 2, slice(c % 2 * wide, c % 2 * wide + wide)
             k.rows_f[me_r, h, :, lanes] = k.grad[c, rows_of(me_r), :]
 
-    def sqb_copy(d):
-        s = (me_b + d) % n_b
-        here = k.sq_b.at[me_b]
-        return remote(here, here, k.sqb_send.at[d], k.sqb_recv.at[me_b], bucket=s)
-
-    def sqb_arrival(d):
-        s = (me_b + d) % n_b
-        here = k.sq_b.at[s]
-        return remote(here, here, k.sqb_send.at[d], k.sqb_recv.at[s], bucket=s)
-
-    def sqr_copy(d):
-        s = (me_r + d) % n_r
-        here = k.sq_r.at[me_r]
-        return remote(here, here, k.sqr_send.at[d], k.sqr_recv.at[me_r], round=s)
-
-    def sqr_arrival(d):
-        s = (me_r + d) % n_r
-        here = k.sq_r.at[s]
-        return remote(here, here, k.sqr_send.at[d], k.sqr_recv.at[s], round=s)
-
-    def back_copy(r):
+    me = me_r * n_b + me_b
+
+    def square_copy(dr, db):
+        here = k.sq_all.at[me]
         return remote(
-            k.back_q.at[r], k.back_in.at[me_r], k.back_send.at[r], k.back_recv.at[me_r], round=r
+            here,
+            here,
+            k.sq_send.at[dr * n_b + db],
+            k.sq_recv.at[me],
+            round=(me_r + dr) % n_r,
+            bucket=(me_b + db) % n_b,
         )
 
+    def square_arrival(dr, db):
+        s = (me_r + dr) % n_r * n_b + (me_b + db) % n_b
+        here = k.sq_all.at[s]
+        return remote(here, here, k.sq_send.at[0], k.sq_recv.at[s], bucket=sibling)
+
+    others = [(dr, db) for dr in range(n_r) for db in range(n_b) if dr or db]
+
+    def back_copy(r, i):
+        return remote(
+            k.back_q.at[r, i],
+            k.back_in.at[me_r, i],
+            k.back_send.at[r, i],
+            k.back_recv.at[me_r, i],
+            round=r,
+        )
+
     def back_arrival(s):
-        here = k.back_in.at[s]
-        return remote(here, here, k.back_send.at[s], k.back_recv.at[s], round=s)
+        for i in range(2):
+
+            def wait():
+                here = k.back_in.at[s, i]
+                remote(
+                    here, here, k.back_send.at[s, i], k.back_recv.at[s, i], round=s
+                ).wait_recv()
+
+            if i == 0:
+                wait()
+            else:
+                pl.when(me_r > 0)(wait)
+
+    def back_drain(s):
+        back_copy(s, 0).wait_send()
+
+        @pl.when(s > 0)
+        def _():
+            back_copy(s, 1).wait_send()
+
+    def give_back(r, i, value):
+        code = jnp.floor(value * top_code + 0.5).astype(jnp.int32) - shift_code
+        k.back_q[r, i] = code.astype(jnp.int16)
+
+        @pl.when(me_r != r)
+        def _():
+            back_copy(r, i).start()
+
+        @pl.when(me_r == r)
+        def _():
+            k.back_in[me_r, i] = k.back_q[r, i]
 
     def prox(sign, factor, after_scale=None):
-        for d in range(1, n_b):
-            sqb_copy(d).start()
+        k.sq_all[me] = jnp.sum(k.sq_mine[...], axis=0, keepdims=True)
+        for dr, db in others:
+            square_copy(dr, db).start()
         for u in range(2):
             for d in range(1, n_r):
                 row_arrival(d, u)
-        for d in range(1, n_b):
-            sqb_arrival(d).wait_recv()
-        k.sq_r[me_r] = jnp.sum(k.sq_b[...], axis=0)
-        for d in range(1, n_r):
-            sqr_copy(d).start()
         for d in range(1, n_r):
             row_arrival(d, 2)
-        for d in range(1, n_r):
-            sqr_arrival(d).wait_recv()
-        squares = jnp.sum(jnp.sum(k.sq_r[...], axis=0), axis=0, keepdims=True)
+        for dr, db in others:
+            square_arrival(dr, db).wait_recv()
+        squares = jnp.sum(k.sq_all[...], axis=0)
         squares = jnp.sum(squares, axis=1, keepdims=True)
         scale = sign / (factor * jnp.sqrt(squares / total_count + epsilon))
 
         if after_scale is not None:
             after_scale()
         carried = None
-        shares = [None] * n_r
         for r in reversed(range(n_r)):
             norms = []
-            shares[r] = []
+            evens = []
             for h in range(2):
                 values = k.rows_f[r, h] * scale
                 if carried is not None:
@@ -412,59 +443,51 @@
                 larger = 1.0 / (1.0 + small)
                 smaller = small * larger
                 ahead = even >= odd
-                k.share[r, h, :, :wide] = jnp.where(ahead, larger, smaller)
+                evens.append(jnp.where(ahead, larger, smaller))
+                k.share[r, h, :, :wide] = evens[h]
                 k.share[r, h, :, wide:] = jnp.where(ahead, smaller, larger)
                 norms.append(jnp.maximum(even, odd) + jnp.log(1.0 + small))
+            give_back(r, 0, jnp.concatenate(evens, axis=1))
             if r > 0:
                 norm = jnp.concatenate(norms, axis=1)
                 carried = picked(split3(norm), k.spread[r - 1])
 
-        mass = None
-        for r in range(n_r):
-            halves = []
-            if r > 0:
-                parent = picked(split3(mass), k.gather[r - 1])
-            for h in range(2):
-                now = k.share[r, h]
-                if r > 0:
-                    above = parent[:, h * wide : (h + 1) * wide]
-                    now = now * jnp.concatenate([above, above], axis=1)
-                halves.append(now)
-            mass = jnp.concatenate(halves, axis=1)
-            code = jnp.floor(mass * top_code + 0.5).astype(jnp.int32) - shift_code
-            k.back_q[r] = code.astype(jnp.int16)
-
-            @pl.when(me_r != r)
-            def _():
-                back_copy(r).start()
-
-            @pl.when(me_r == r)
-            def _():
-                k.back_in[me_r] = k.back_q[r]
+        mass = jnp.concatenate([k.share[0, 0], k.share[0, 1]], axis=1)
+        for r in range(1, n_r):
+            parent = picked(split3(mass), k.gather[r - 1])
+            give_back(r, 1, parent)
+            above = [parent[:, h * wide : (h + 1) * wide] for h in (0, 0, 1, 1)]
+            shares = jnp.concatenate([k.share[r, 0], k.share[r, 1]], axis=1)
+            mass = shares * jnp.concatenate(above, axis=1)
 
     def prox_drain():
         for d in range(1, n_r):
             for u in range(3):
                 row_copy(d, u).wait_send()
-            back_copy((me_r + d) % n_r).wait_send()
-            sqr_copy(d).wait_send()
-        for d in range(1, n_b):
-            sqb_copy(d).wait_send()
+            back_drain((me_r + d) % n_r)
+        for dr, db in others:
+            square_copy(dr, db).wait_send()
 
     def pieces(s):
-        whole = (k.back_in[s].astype(jnp.int32) + shift_code).astype(f32)
-        hi = whole.astype(bf16)
-        return [hi, (whole - hi.astype(f32)).astype(bf16)]
+        share, parent = [
+            (k.back_in[s, i].astype(jnp.int32) + shift_code).astype(f32) * (1.0 / top_code)
+            for i in range(2)
+        ]
+        even = parent * share
+        odd = parent - even
+        both = (even[:, :wide], odd[:, :wide], even[:, wide:], odd[:, wide:])
+        whole = jnp.concatenate(both, axis=1)
+        return split3(whole)[:2]
 
     def mixed_part(s, state, weight, dims):
         value = mix(pieces(s), [k.mix_p[i] for i in range(3)], dims)
-        value = (1.0 - weight) * state[rows_of(s), :] + (weight * (1.0 / top_code)) * value
+        value = (1.0 - weight) * state[rows_of(s), :] + weight * value
         state[rows_of(s), :] = value
         return value
 
     def add_best(out, s, share):
         best = picked(pieces(s), k.to_outer[...])
-        out[0, rows_of(s), :] += (share * (1.0 / top_code)) * best
+        out[0, rows_of(s), :] += share * best
 
 
     def mixed_copy(s):
@@ -751,7 +774,7 @@
         for d in range(n_r):
             s = (me_r + d) % n_r
             if d > 0:
-                back_arrival(s).wait_recv()
+                back_arrival(s)
             value = mixed_part(s, k.f_x, weight, nn).astype(bf16)
             for c in range(4):
                 k.mixed[core, c, rows_of(s), :] = value[:, c * wide : (c + 1) * wide]
@@ -803,7 +826,7 @@
         for d in range(n_r):
             s = (me_r + d) % n_r
             if d > 0:
-                back_arrival(s).wait_recv()
+                back_arrival(s)
 
             @pl.when(index == 0)
             def _():
@@ -869,10 +892,10 @@
         row_in=pltpu.VMEM((n_r, 4, part + 16, half // 2), i16),
         rows_f=pltpu.VMEM((n_r, 2, part, half), f32),
         share=pltpu.VMEM((n_r, 2, part, half), f32),
-        back_q=pltpu.VMEM((n_r, part, seqs), i16),
-        back_in=pltpu.VMEM((n_r, part, seqs), i16),
-        sq_b=pltpu.VMEM((n_b, 8, 128), f32),
-        sq_r=pltpu.VMEM((n_r, 8, 128), f32),
+        back_q=pltpu.VMEM((n_r, 2, part, half), i16),
+        back_in=pltpu.VMEM((n_r, 2, part, half), i16),
+        sq_mine=pltpu.VMEM((8, 128), f32),
+        sq_all=pltpu.VMEM((n_r * n_b, 1, 128), f32),
         load_sem=dma((3,)),
         out_sem=dma((2, n_r)),
         turn_send=dma((pairs,)),
@@ -893,12 +916,10 @@
         raw_recv=dma((2, 4)),
         row_send=dma((n_r, 3)),
         row_recv=dma((n_r, 3)),
-        back_send=dma((n_r,)),
-        back_recv=dma((n_r,)),
-        sqb_send=dma((n_b,)),
-        sqb_recv=dma((n_b,)),
-        sqr_send=dma((n_r,)),
-        sqr_recv=dma((n_r,)),
+        back_send=dma((n_r, 2)),
+        back_recv=dma((n_r, 2)),
+        sq_send=dma((n_r * n_b,)),
+        sq_recv=dma((n_r * n_b,)),
     )
     names = ["x_hbm", "y_hbm", "pay_hbm", "col_ref", "coef_ref", "pred_ref", "x_out", "y_out"]
     names += list(scratch)

time: 220 us -> 210 us (0.955)
  Pallas kernels: 218 us -> 207 us
    pallas_call x1, Pallas kernels: 215 us -> 205 us  [line_body(): pl.pallas_call(functools.partial(line_kernel, names, n_r, n_b), out_shape...]
where the time goes in v4:
time: 210 us; the launch traced here: 209 us
  Pallas kernels  207 us (99%)
    pallas_call x1, Pallas kernels, line_body(): pl.pallas_call(functools.partial(line_kernel, names, n_r, n_b), out_shape...  205 us

profile of v4, /device:TPU:0, one launch (start us, length us, event | category | flops | bytes accessed | tf_op | source)
XLA Modules:
  0.0 209.2 jit_solution(8895777609841067005)
XLA Ops:
  0.6 1.3 copy.8.refs_3_
  2.0 204.6 %shard_map.77 = (f32[1,512,512]{2,1,0:T(8,128)}, f32[1,512,512]{2,1,0:T(8,128)}) custom-call(f32[1,512,512]{2,1,0:T(8,128)} %refs_0_.1, f32[1,512,512]{2,1,0:T(8,128)} %refs_1_.1, bf16[1,512,4096]{2,1,0:T(8,128)(2,1)} %refs_2_.1, s32[1,4,3]{2,1,0:T(4,128)} %copy.8.refs_3_, f32[1,4,3,128,128]{4,3,2,1,0:T(8,128)} %refs_4_.1, s32[3,256]{1,0:T(4,128)} %refs_5_.1), custom_call_target="tpu_custom_call" | custom-call | tf_op jit(solution)/shard_map/pallas_call | solution.py:926
  206.6 2.6 %shard_map.78 = (f32[1,512,512]{2,1,0:T(8,128)}, f32[1,512,512]{2,1,0:T(8,128)}) custom-call(f32[1,512,512]{2,1,0:T(8,128)} %get-tuple-element.4.x_in, f32[1,512,512]{2,1,0:T(8,128)} %get-tuple-element.5.y_in), custom_call_target="tpu_custom_call" | custom-call | tf_op jit(solution)/shard_map/pallas_call | solution.py:937

commit v5 on v4

--- a/solution.py
+++ b/solution.py
@@ -142,7 +142,7 @@
         for c in range(tiles):
             value = jnp.zeros((tile, tile), f32)
             for t in range(per_row):
-                value = value + jnp.where(k.col_ref[0, m, t] == c, k.coef_ref[0, m, t], 0.0)
+                value = value + jnp.where(k.col_ref[t, 0, m] == c, k.coef_ref[0, m, t], 0.0)
             k.mixer[m * tile : (m + 1) * tile, c * tile : (c + 1) * tile] = value
     for i, piece in enumerate(split3(k.mixer[...])):
         k.mix_p[i] = dot(k.to_outer[...], piece).astype(bf16)
@@ -336,11 +336,6 @@
         k.rows_f[s, h, :, lanes] = decode(here)
 
     def finish(u):
-        for d in range(1, n_r):
-            s = (me_r + d) % n_r
-            for c in members[u]:
-                encode(k.grad[c, rows_of(s), :], k.row_q.at[s, c])
-            row_copy(d, u).start()
         for c in members[u]:
             squares = k.grad[c]
             squares = jnp.sum((squares * squares).reshape(rows // 8, 8, wide), axis=0)
@@ -348,6 +343,16 @@
                 k.sq_mine[...] = squares
             else:
                 k.sq_mine[...] += squares
+        if u == 2:
+            k.sq_all[me] = jnp.sum(k.sq_mine[...], axis=0, keepdims=True)
+            for dr, db in others:
+                square_copy(dr, db).start()
+        for d in range(1, n_r):
+            s = (me_r + d) % n_r
+            for c in members[u]:
+                encode(k.grad[c, rows_of(s), :], k.row_q.at[s, c])
+            row_copy(d, u).start()
+        for c in members[u]:
             h, lanes = c // 2, slice(c % 2 * wide, c % 2 * wide + wide)
             k.rows_f[me_r, h, :, lanes] = k.grad[c, rows_of(me_r), :]
 
@@ -414,9 +419,6 @@
             k.back_in[me_r, i] = k.back_q[r, i]
 
     def prox(sign, factor, after_scale=None):
-        k.sq_all[me] = jnp.sum(k.sq_mine[...], axis=0, keepdims=True)
-        for dr, db in others:
-            square_copy(dr, db).start()
         for u in range(2):
             for d in range(1, n_r):
                 row_arrival(d, u)
@@ -540,9 +542,6 @@
         return decode(here)
 
     def sums_of_end(index):
-        for n in range(4):
-            raw_copy(n).start()
-
         def lend_sum(n, _):
             k.work[...] = partial(facing - outward // 2, n)
             encode(k.work[...], k.sum_out.at[4, n])
@@ -779,6 +778,12 @@
             for c in range(4):
                 k.mixed[core, c, rows_of(s), :] = value[:, c * wide : (c + 1) * wide]
             mixed_copy(s).start()
+
+        @pl.when(jnp.logical_not(inner))
+        def _():
+            for n in range(4):
+                raw_copy(n).start()
+
         for d in range(n_r):
             mixed_arrival((me_r + d) % n_r).wait_recv()
 
@@ -932,7 +937,14 @@
         compiler_params=pltpu.CompilerParams(
             collective_id=0, has_side_effects=True, vmem_limit_bytes=60 * 1024 * 1024
         ),
-    )(x_start, y_start, bucket_payoff, column_blocks, public_coef, predecessor_sequences)
+    )(
+        x_start,
+        y_start,
+        bucket_payoff,
+        jnp.transpose(column_blocks, (2, 0, 1)),
+        public_coef,
+        predecessor_sequences,
+    )
     block = pl.BlockSpec((1, rows // 2, seqs), lambda i: (0, i, 0))
     return pl.pallas_call(
         place_kernel,

time: 210 us -> 208 us (level)
  no operation moved by 1% of the time
where the time goes in v5:
time: 208 us; the launch traced here: 207 us
  Pallas kernels  207 us (100%)
    pallas_call x1, Pallas kernels, line_body(): pl.pallas_call(functools.partial(line_kernel, names, n_r, n_b), out_shape...  204 us

profile of v5, /device:TPU:0, one launch (start us, length us, event | category | flops | bytes accessed | tf_op | source)
XLA Modules:
  0.0 207.5 jit_solution(17534538599596129780)
XLA Ops:
  0.6 204.2 %shard_map.77 = (f32[1,512,512]{2,1,0:T(8,128)}, f32[1,512,512]{2,1,0:T(8,128)}) custom-call(f32[1,512,512]{2,1,0:T(8,128)} %refs_0_.1, f32[1,512,512]{2,1,0:T(8,128)} %refs_1_.1, bf16[1,512,4096]{2,1,0:T(8,128)(2,1)} %refs_2_.1, s32[3,1,4]{2,1,0:T(1,128)} %bitcast.1, f32[1,4,3,128,128]{4,3,2,1,0:T(8,128)} %refs_4_.1, s32[3,256]{1,0:T(4,128)} %refs_5_.1), custom_call_target="tpu_custom_call" | custom-call | tf_op jit(solution)/shard_map/pallas_call | solution.py:931
  204.9 2.6 %shard_map.78 = (f32[1,512,512]{2,1,0:T(8,128)}, f32[1,512,512]{2,1,0:T(8,128)}) custom-call(f32[1,512,512]{2,1,0:T(8,128)} %get-tuple-element.4.x_in, f32[1,512,512]{2,1,0:T(8,128)} %get-tuple-element.5.y_in), custom_call_target="tpu_custom_call" | custom-call | tf_op jit(solution)/shard_map/pallas_call | solution.py:949

commit v6 on v5

--- a/solution.py
+++ b/solution.py
@@ -185,7 +185,7 @@
             bucket=sibling,
         )
 
-    def take_lent(o):
+    def wait_lent(o):
         j = lent_place(o)
         for i in range(2):
             for p in range(2):
@@ -194,6 +194,9 @@
                 remote(
                     here, here, k.lend_send.at[turn], k.lend_recv.at[turn], bucket=sibling
                 ).wait_recv()
+
+    def turn_lent(o):
+        j = lent_place(o)
         k.pay_out[j] = k.lent[2 * j + 1 - core].T
         lent_swap(j, o).start()
         k.lent_t[j, core] = k.lent[2 * j + core].T
@@ -682,6 +685,12 @@
 
         both(first)
 
+        @pl.when(inner & jnp.logical_not(plain))
+        def _():
+            wait_lent(1)
+            for c in range(4):
+                k.early[c] = lent_product(b, c) + lent_product(sibling + first, c)
+
         @pl.when(jnp.logical_not(inner) & plain)
         def _():
             by_parts(b2)
@@ -690,12 +699,6 @@
         @pl.when(inner | plain)
         def _():
             both(second)
-
-        @pl.when(inner & jnp.logical_not(plain))
-        def _():
-            take_lent(1)
-            for c in range(4):
-                k.early[c] = lent_product(b, c) + lent_product(sibling + first, c)
 
         b3 = me_b + far
         for c in range(4):
@@ -731,6 +734,10 @@
 
             if c > 0:
                 finish(c - 1)
+
+        @pl.when(inner & jnp.logical_not(plain))
+        def _():
+            turn_lent(1)
 
         @pl.when(inner & plain)
         def _():
@@ -791,7 +798,8 @@
         def _():
             @pl.when(index == 0)
             def _():
-                take_lent(0)
+                wait_lent(0)
+                turn_lent(0)
 
             sums_of_inner(index)
 

time: 208 us -> 207 us (level)
  no operation moved by 1% of the time
where the time goes in v6:
time: 207 us
  Pallas kernels  206 us (100%)
    pallas_call x1, Pallas kernels, line_body(): pl.pallas_call(functools.partial(line_kernel, names, n_r, n_b), out_shape...  203 us

profile of v6, /device:TPU:0, one launch (start us, length us, event | category | flops | bytes accessed | tf_op | source)
XLA Modules:
  0.0 206.6 jit_solution(10312599090074701489)
XLA Ops:
  0.6 203.3 %shard_map.77 = (f32[1,512,512]{2,1,0:T(8,128)}, f32[1,512,512]{2,1,0:T(8,128)}) custom-call(f32[1,512,512]{2,1,0:T(8,128)} %refs_0_.1, f32[1,512,512]{2,1,0:T(8,128)} %refs_1_.1, bf16[1,512,4096]{2,1,0:T(8,128)(2,1)} %refs_2_.1, s32[3,1,4]{2,1,0:T(1,128)} %bitcast.1, f32[1,4,3,128,128]{4,3,2,1,0:T(8,128)} %refs_4_.1, s32[3,256]{1,0:T(4,128)} %refs_5_.1), custom_call_target="tpu_custom_call" | custom-call | tf_op jit(solution)/shard_map/pallas_call | solution.py:939
  204.0 2.6 %shard_map.78 = (f32[1,512,512]{2,1,0:T(8,128)}, f32[1,512,512]{2,1,0:T(8,128)}) custom-call(f32[1,512,512]{2,1,0:T(8,128)} %get-tuple-element.4.x_in, f32[1,512,512]{2,1,0:T(8,128)} %get-tuple-element.5.y_in), custom_call_target="tpu_custom_call" | custom-call | tf_op jit(solution)/shard_map/pallas_call | solution.py:957

commit v7 on v6

--- a/solution.py
+++ b/solution.py
@@ -378,6 +378,7 @@
         return remote(here, here, k.sq_send.at[0], k.sq_recv.at[s], bucket=sibling)
 
     others = [(dr, db) for dr in range(n_r) for db in range(n_b) if dr or db]
+    others.sort(key=lambda o: -min(o[1], n_b - o[1]))
 
     def back_copy(r, i):
         return remote(

time: 207 us -> 207 us (level)
  no operation moved by 1% of the time
where the time goes in v7:
time: 207 us; the launch traced here: 206 us
  Pallas kernels  206 us (100%)
    pallas_call x1, Pallas kernels, line_body(): pl.pallas_call(functools.partial(line_kernel, names, n_r, n_b), out_shape...  203 us

profile of v7, /device:TPU:0, one launch (start us, length us, event | category | flops | bytes accessed | tf_op | source)
XLA Modules:
  0.0 206.4 jit_solution(16849516512929400678)
XLA Ops:
  0.6 203.2 %shard_map.77 = (f32[1,512,512]{2,1,0:T(8,128)}, f32[1,512,512]{2,1,0:T(8,128)}) custom-call(f32[1,512,512]{2,1,0:T(8,128)} %refs_0_.1, f32[1,512,512]{2,1,0:T(8,128)} %refs_1_.1, bf16[1,512,4096]{2,1,0:T(8,128)(2,1)} %refs_2_.1, s32[3,1,4]{2,1,0:T(1,128)} %bitcast.1, f32[1,4,3,128,128]{4,3,2,1,0:T(8,128)} %refs_4_.1, s32[3,256]{1,0:T(4,128)} %refs_5_.1), custom_call_target="tpu_custom_call" | custom-call | tf_op jit(solution)/shard_map/pallas_call | solution.py:940
  203.9 2.6 %shard_map.78 = (f32[1,512,512]{2,1,0:T(8,128)}, f32[1,512,512]{2,1,0:T(8,128)}) custom-call(f32[1,512,512]{2,1,0:T(8,128)} %get-tuple-element.4.x_in, f32[1,512,512]{2,1,0:T(8,128)} %get-tuple-element.5.y_in), custom_call_target="tpu_custom_call" | custom-call | tf_op jit(solution)/shard_map/pallas_call | solution.py:958
